TPU v7x, 256 devices: a whole 4x4x8 slice. The times are simulated.
256 devices in a mesh: dp: 8 (over y, core), expert: 32 (over z, x).
Axes of the slice: x: 4, y: 4, z: 8, core: 2. Of those that a mesh axis runs over, the one named last changes fastest.
Arguments:
- frames_in: bfloat16 [256, 256, 1024], P(('dp', 'expert')), may hold values from -6 to 6
- pit_order: int32 [128, 2], replicated, may hold values from 0 to 1, each once within a row
- expert_ids: int32 [256, 256, 2], P(('dp', 'expert')), may hold values from 0 to 31, all different within a row; in each aligned block of 256 rows (0 to 255, 256 to 511, ..., all dimensions but the last counted through in order) at most 20 rows name the same one
- norm_gains: float32 [2, 1024], replicated, may hold values from 0.25 to 1.75
- attn_qkv: bfloat16 [3, 1024, 1024], P(None, 'expert'), may hold values from -6 to 6
- attn_out: bfloat16 [1024, 1024], P('expert'), may hold values from -0.1875 to 0.1875
- router: float32 [1024, 32], replicated, may hold values from -0.046875 to 0.046875
- expert_in: bfloat16 [32, 1024, 4096], P('expert', None, 'dp'), may hold values from -0.1875 to 0.1875
- expert_out: bfloat16 [32, 4096, 1024], P('expert', 'dp'), may hold values from -0.09375 to 0.09375
Outputs:
- layer_out: bfloat16 [256, 256, 1024], P(('dp', 'expert'))
Inputs may be any that keep to these rules, and one draw needn't show every extreme that they name: `expert_ids`: at most 20 frames of one stream name the same expert, and in every draw some stream names some expert exactly 20 times; each frame names 2 different experts.
All inputs are finite; a program needn't handle non-finite values.
Results may differ from a plain program's by a relative error of at most 0.011.
Values may be sent and summed in bfloat16 or wider, within the bound.
A program may use at most 128 MiB of HBM per device.

v0:
```python
import jax
import jax.numpy as jnp
from jax import lax
from jax.sharding import PartitionSpec as P

HEAD_DIM = 64


epsilon = 1e-05


def from_partner(block, axis, bit):
    count = lax.axis_size(axis)
    route = []
    for low in range(count):
        high = low | 1 << bit
        if high != low and high < count:
            route += [(low, high), (high, low)]
    return lax.ppermute(block, axis, route)


def layer_norm(values, gain):
    mean = jnp.mean(values, axis=-1, keepdims=True)
    centred = values - mean
    spread = jnp.mean(centred * centred, axis=-1, keepdims=True)
    return centred * lax.rsqrt(spread + epsilon) * gain


def body(
    frames_in, pit_order, expert_ids, norm_gains, attn_qkv, attn_out, router, expert_in, expert_out
):
    dp_count = lax.axis_size("dp")
    exp_count = lax.axis_size("expert")
    dp_index = lax.axis_index("dp")
    exp_index = lax.axis_index("expert")
    frames = frames_in.shape[1]
    width = frames_in.shape[2]
    heads = width // HEAD_DIM
    top = expert_ids.shape[2]
    capacity = frames * top * 5 // (4 * exp_count)
    partner = from_partner(frames_in, "dp", dp_count.bit_length() - 2)
    half = dp_count // 2
    speaker = dp_index // half
    meeting = dp_index % half * exp_count + exp_index
    source = pit_order[meeting, speaker]
    stream = jnp.where(source == speaker, frames_in[0], partner[0])
    resid = stream.astype(jnp.float32)
    normed = layer_norm(resid, norm_gains[0]).astype(jnp.bfloat16)
    columns = normed
    projected = jnp.einsum(
        "fc,jcd->jfd",
        columns,
        lax.all_gather(attn_qkv, "expert", axis=1, tiled=True),
        preferred_element_type=jnp.float32,
    )
    projected = projected.astype(jnp.bfloat16).reshape(3, frames, heads, HEAD_DIM)
    scores = (
        jnp.einsum("qhd,khd->hqk", projected[0], projected[1], preferred_element_type=jnp.float32)
        / HEAD_DIM**0.5
    )
    highest = jnp.max(scores, axis=-1, keepdims=True)
    weights = jnp.exp(scores - highest)
    probs = (weights / jnp.sum(weights, axis=-1, keepdims=True)).astype(jnp.bfloat16)
    context = jnp.einsum("hqk,khd->qhd", probs, projected[2], preferred_element_type=jnp.float32)
    context = context.reshape(frames, width).astype(jnp.bfloat16)
    columns = context
    attended = jnp.dot(
        columns,
        lax.all_gather(attn_out, "expert", axis=0, tiled=True),
        preferred_element_type=jnp.float32,
    )
    mixed = (resid + attended).astype(jnp.bfloat16)
    mixed_wide = mixed.astype(jnp.float32)
    normed2 = layer_norm(mixed_wide, norm_gains[1]).astype(jnp.bfloat16)
    logits = jnp.dot(normed2.astype(jnp.float32), router, precision=lax.Precision.HIGHEST)
    chosen = expert_ids[0]
    picked = jnp.take_along_axis(logits, chosen, axis=1)
    gate_first = jax.nn.sigmoid(picked[:, 0] - picked[:, 1])
    gate_second = 1.0 - gate_first
    flat = chosen.reshape(-1)
    onehot = (flat[:, None] == jnp.arange(exp_count, dtype=jnp.int32)[None, :]).astype(jnp.int32)
    ranks = jnp.sum(onehot * (jnp.cumsum(onehot, axis=0) - 1), axis=1)
    positions = flat * capacity + ranks
    rows = jnp.repeat(normed2, top, axis=0)
    outgoing = jnp.zeros((exp_count * capacity, width), jnp.bfloat16).at[positions].set(rows)
    outgoing = outgoing.reshape(exp_count, capacity, width)
    piece = lax.all_gather(
        lax.all_to_all(outgoing, "expert", split_axis=0, concat_axis=0, tiled=True),
        "dp",
        axis=0,
        tiled=True,
    )
    flat_rows = piece.reshape(-1, piece.shape[-1])
    hidden = jax.nn.silu(
        jnp.dot(flat_rows, expert_in[0], preferred_element_type=jnp.float32)
    ).astype(jnp.bfloat16)
    partials = (
        jnp.dot(hidden, expert_out[0], preferred_element_type=jnp.float32)
        .astype(jnp.bfloat16)
        .reshape(piece.shape)
    )
    summed = lax.psum_scatter(partials, "dp", scatter_dimension=0, tiled=True).astype(jnp.float32)
    answer = summed.astype(jnp.bfloat16)
    returned = lax.all_to_all(answer, "expert", split_axis=0, concat_axis=0, tiled=True)
    back = returned.reshape(exp_count * capacity, width)[positions]
    back = back.reshape(frames, top, width).astype(jnp.float32)
    result = mixed_wide + gate_first[:, None] * back[:, 0] + gate_second[:, None] * back[:, 1]
    return result.astype(jnp.bfloat16)[None]


def solution(mesh):
    return jax.shard_map(
        body,
        mesh=mesh,
        in_specs=(
            P(("dp", "expert"), None, None),
            P(),
            P(("dp", "expert"), None, None),
            P(),
            P(None, "expert", None),
            P("expert", None),
            P(),
            P("expert", None, "dp"),
            P("expert", "dp", None),
        ),
        out_specs=P(("dp", "expert"), None, None),
        check_vma=False,
    )
```

profile of v0, /device:TPU:1, one launch (start us, length us, event | category | flops | bytes accessed | tf_op | source)
XLA Modules:
  0.0 494.1 jit_solution(15275122537670167731)
XLA Ops:
  8.1 3.8 collective-permute-start
  18.3 4.5 collective-permute-done
  23.3 78.7 %all-gather.4.cloned.1.call-done = bf16[3,1024,1024]{2,1,0:T(8,128)(2,1)} async-done(((bf16[3,32,1024]{2,1,0:T(8,128)(2,1)}), bf16[3,1024,1024]{2,1,0:T(8,128)(2,1)}) %all-gather.4.cloned.1.call-update) | async-done | bytes 6291472 | tf_op jit(solution)/shard_map/all_gather | solution.py:53
  102.1 4.7 fusion.7
  108.3 4.5 fusion.58
  112.8 2.7 fusion.10
  115.5 60.5 %all-gather.6.cloned.1.call-done = bf16[1024,1024]{1,0:T(8,128)(2,1)} async-done(((bf16[32,1024]{1,0:T(8,128)(2,1)}), bf16[1024,1024]{1,0:T(8,128)(2,1)}) %all-gather.6.cloned.1.call-update) | async-done | bytes 2097168 | tf_op jit(solution)/shard_map/all_gather | solution.py:69
  176.0 2.4 convert_reduce_fusion
  181.3 4.4 scatter_custom_fusion
  185.7 2.2 reshape.141
  187.9 39.2 %all_to_all.10 = bf16[32,20,1024]{2,1,0:T(8,128)(2,1)S(1)} all-to-all(bf16[32,20,1024]{2,1,0:T(8,128)(2,1)S(1)} %reshape.141), channel_id=1, replica_groups=mesh['dp'=8,'expert'=32] {'expert'}, dimensions={0} | all-to-all | bytes 2621440 | tf_op jit(solution)/shard_map/all_to_all | solution.py:88
  227.1 1.8 copy.48
  228.9 63.8 %all-gather.8.cloned.1.call-done = bf16[256,20,1024]{2,0,1:T(8,128)(2,1)} async-done(((bf16[32,20,1024]{2,0,1:T(8,128)(2,1)}), bf16[256,20,1024]{2,0,1:T(8,128)(2,1)}) %all-gather.8.cloned.1.call-update) | async-done | bytes 10485776 | tf_op jit(solution)/shard_map/all_gather | solution.py:87
  292.7 14.1 %copy.49 = bf16[256,20,1024]{2,1,0:T(8,128)(2,1)} copy(bf16[256,20,1024]{2,0,1:T(8,128)(2,1)} %all-gather.8.cloned.1.call-done) | data formatting | bytes 20971520 | tf_op jit(solution)/shard_map/all_gather | solution.py:87
  306.8 16.5 %reshape.142 = bf16[5120,1024]{1,0:T(8,128)(2,1)} reshape(bf16[256,20,1024]{2,1,0:T(8,128)(2,1)} %copy.49) | data formatting | bytes 20971520 | tf_op jit(solution)/shard_map/reshape | solution.py:93
  323.4 17.1 %convolution_convert_fusion = bf16[5120,1024]{1,0:T(8,128)(2,1)} fusion(bf16[1,512,1024]{2,1,0:T(8,128)(2,1)S(1)} %copy-done, bf16[5120,1024]{1,0:T(8,128)(2,1)} %reshape.142, bf16[1,1024,512]{2,1,0:T(8,128)(2,1)S(1)} %copy-done.6), kind=kOutput, calls=%fused_computation.5 | convolution fusion | flops 10755768320 | bytes 23068672 | tf_op jit(solution)/shard_map/dot_general | solution.py:98
  340.4 16.3 %reshape.143 = bf16[256,20,1024]{2,1,0:T(8,128)(2,1)} reshape(bf16[5120,1024]{1,0:T(8,128)(2,1)} %convolution_convert_fusion) | data formatting | bytes 20971520 | tf_op jit(solution)/shard_map/reshape | solution.py:100
  356.8 74.4 %reduce-scatter.2.cloned.1.call-done = bf16[32,20,1024]{2,1,0:T(8,128)(2,1)} async-done(((bf16[256,20,1024]{2,1,0:T(8,128)(2,1)}), bf16[32,20,1024]{2,1,0:T(8,128)(2,1)}) %reduce-scatter.2.cloned.1.call-update) | async-done | bytes 1310736 | tf_op jit(solution)/shard_map/reduce_scatter | solution.py:102
  431.2 9.9 %all-to-all-start.1 = ((bf16[32,20,1024]{2,1,0:T(8,128)(2,1)}), bf16[32,20,1024]{2,1,0:T(8,128)(2,1)}, u32[]{:S(2)}, u32[]{:S(2)}) async-start(bf16[32,20,1024]{2,1,0:T(8,128)(2,1)} %reduce-scatter.2.cloned.1.call-done), calls=%async_computation.2 | async-start | bytes 3145728 | tf_op jit(solution)/shard_map/all_to_all | solution.py:104
  442.0 4.5 gather_fusion.1
  447.0 30.1 %all-to-all-done.1 = bf16[32,20,1024]{2,1,0:T(8,128)(2,1)} async-done(((bf16[32,20,1024]{2,1,0:T(8,128)(2,1)}), bf16[32,20,1024]{2,1,0:T(8,128)(2,1)}, u32[]{:S(2)}, u32[]{:S(2)}) %all-to-all-start.1) | async-done | bytes 1310752 | tf_op jit(solution)/shard_map/all_to_all | solution.py:104
  477.1 2.3 reshape.144
  479.4 2.8 gather_fusion
  482.2 2.5 reshape.145
  (61 shorter events, 16.3 us)
Async XLA Ops:
  6.5 316.8 %copy-start = (bf16[1,512,1024]{2,1,0:T(8,128)(2,1)S(1)}, bf16[1,512,1024]{2,1,0:T(8,128)(2,1)}, u32[]{:S(2)}) copy-start(bf16[1,512,1024]{2,1,0:T(8,128)(2,1)} %param.17) | copy-start | bytes 3145732
  6.5 95.5 %all-gather.4.cloned.1.call-start = ((), (), s32[]{:S(2)}) async-start(), calls=%async_computation.3 | async-start | bytes 6488064 | tf_op jit(solution)/shard_map/all_gather | solution.py:53
  7.3 168.7 %all-gather.6.cloned.1.call-start = ((), (), s32[]{:S(2)}) async-start(), calls=%async_computation.4 | async-start | bytes 2162688 | tf_op jit(solution)/shard_map/all_gather | solution.py:69
  8.0 284.7 %all-gather.8.cloned.1.call-start = ((), (), s32[]{:S(2)}) async-start(), calls=%async_computation.5 | async-start | bytes 11796480 | tf_op jit(solution)/shard_map/all_gather | solution.py:87
  8.1 14.7 %collective-permute-start = (bf16[1,256,1024]{2,1,0:T(8,128)(2,1)}, bf16[1,256,1024]{2,1,0:T(8,128)(2,1)S(1)}, u32[]{:S(2)}, u32[]{:S(2)}) collective-permute-start(bf16[1,256,1024]{2,1,0:T(8,128)(2,1)} %param.9), channel_id=1, source_target_pairs={{0,128},{128,0},{32,160},{160,32},{64,192},{192,64},{96,224},{224,... | collective-permute-start | bytes 1572872 | tf_op jit(solution)/shard_map/ppermute | solution.py:19
  178.4 0.8 copy-start.2
  228.9 202.4 %reduce-scatter.2.cloned.1.call-start = ((), (), s32[]{:S(2)}) async-start(), calls=%async_computation.6 | async-start | bytes 14155776 | tf_op jit(solution)/shard_map/reduce_scatter | solution.py:102
  306.8 16.5 %copy-start.6 = (bf16[1,1024,512]{2,1,0:T(8,128)(2,1)S(1)}, bf16[1,1024,512]{2,1,0:T(8,128)(2,1)}, u32[]{:S(2)}) copy-start(bf16[1,1024,512]{2,1,0:T(8,128)(2,1)} %param.16) | copy-start | bytes 3145732
  356.8 84.3 %copy-start.5 = (s32[1,256,2]{1,2,0:T(2,128)S(1)}, s32[1,256,2]{1,2,0:T(2,128)}, u32[]{:S(2)}) copy-start(s32[1,256,2]{1,2,0:T(2,128)} %param.11) | copy-start | bytes 6148
  356.8 84.7 %copy-start.4 = (f32[1024,32]{0,1:T(8,128)S(1)}, f32[1024,32]{0,1:T(8,128)}, u32[]{:S(2)}) copy-start(f32[1024,32]{0,1:T(8,128)} %param.15) | copy-start | bytes 393220
  431.2 45.8 %all-to-all-start.1 = ((bf16[32,20,1024]{2,1,0:T(8,128)(2,1)}), bf16[32,20,1024]{2,1,0:T(8,128)(2,1)}, u32[]{:S(2)}, u32[]{:S(2)}) async-start(bf16[32,20,1024]{2,1,0:T(8,128)(2,1)} %reduce-scatter.2.cloned.1.call-done), calls=%async_computation.2 | async-start | bytes 3145728 | tf_op jit(solution)/shard_map/all_to_all | solution.py:104
  482.2 5.4 %copy-start.1 = (bf16[1,512,1024]{2,1,0:T(8,128)(2,1)S(1)}, bf16[1,512,1024]{2,1,0:T(8,128)(2,1)}, u32[]{:S(2)}) copy-start(bf16[1,512,1024]{2,1,0:T(8,128)(2,1)} %param.17) | copy-start | bytes 3145732
  484.6 1.6 copy-start.3
Sparse Core Ops, SparseCore 0:
  9.9 92.0 all-gather.3
  104.6 71.3 all-gather.5
  229.0 63.6 all-gather.7
  356.9 74.2 reduce-scatter.1
where the time goes:
time: 499 us; the launch traced here: 494 us
  waiting for transfers between devices  313 us (63%)
  local copies, waits for them, and re-layouts  76.9 us (15%)
  blocking collectives  39.2 us (8%)
  matrix products  31.9 us (6%)
  between operations  14.1 us (3%)
  starting transfers between devices  13.8 us (3%)
    all_gather x1, waiting for transfers between devices, body(): lax.all_gather(attn_qkv, 'expert', axis=1, tiled=True)  78.7 us
    reduce_scatter x1, waiting for transfers between devices, body(): lax.psum_scatter(partials, 'dp', scatter_dimension=0, tiled=True)  74.4 us
    all_gather x1, waiting for transfers between devices, body(): lax.all_gather(lax.all_to_all(outgoing, 'expert', split_axis=0, concat_ax...  63.8 us
    all_gather x1, waiting for transfers between devices, body(): lax.all_gather(attn_out, 'expert', axis=0, tiled=True)  60.5 us
    all_to_all x1, blocking collectives, body(): lax.all_to_all(outgoing, 'expert', split_axis=0, concat_axis=0, tiled=True)  39.2 us
    all_to_all x1, waiting for transfers between devices, body(): lax.all_to_all(answer, 'expert', split_axis=0, concat_axis=0, tiled=True)  30.1 us
    dot_general x1, matrix products, body(): jnp.dot(hidden, expert_out[0], preferred_element_type=jnp.float32)  17.1 us
    reshape x1, local copies, waits for them, and re-layouts, body(): flat_rows = piece.reshape(-1, piece.shape[-1])  16.5 us
  transfers between devices with their start and end apart: 6, of which 6 were waited for; matrix products, arithmetic and copies ran while one was open for 5% of the time, Pallas kernels for 0%

commit v1 on v0

v1 whole, which is shorter than its diff:
```python
import jax
import jax.numpy as jnp
from jax import lax
from jax.experimental import pallas as pl
from jax.experimental.pallas import tpu as pltpu
from jax.sharding import PartitionSpec as P

HEAD_DIM = 64
MESH = pl.DeviceIdType.MESH
BF = jnp.bfloat16
F32 = jnp.float32

NX, NZ, NY = 4, 8, 4
NE = NX * NZ
F = 256
D = 1024
H = 512
R = 16
CAP = 20
X = 256
epsilon = 1e-05


def layer_norm(values, gain):
    mean = jnp.mean(values, axis=-1, keepdims=True)
    centred = values - mean
    spread = jnp.mean(centred * centred, axis=-1, keepdims=True)
    return centred * lax.rsqrt(spread + epsilon) * gain


def dot(a, b):
    return jnp.dot(a, b, preferred_element_type=F32)


def iota(shape, dim):
    return lax.broadcasted_iota(jnp.int32, shape, dim)


def onehot(mask):
    return jnp.where(mask, 1.0, 0.0).astype(BF)


def kernel(
    keep,
    ids,
    ids_t,
    gains,
    router,
    frames,
    qkv,
    wo,
    win,
    wout,
    out,
    pbuf,
    strm,
    normed,
    wall,
    wo_sib,
    proj,
    ctxh,
    ctxs,
    mixed,
    tx,
    rx,
    ry,
    fx,
    xr,
    acc,
    win_all,
    wout_all,
    pick,
    pick_x,
    ring_s,
    ring_r,
    w_s,
    w_r,
    m_s,
    m_r,
    t_s,
    t_r,
    f_s,
    f_r,
    loc,
):
    dp = lax.axis_index("dp")
    ex = lax.axis_index("expert")
    y, c = lax.div(dp, 2), lax.rem(dp, 2)
    z, x = lax.div(ex, NX), lax.rem(ex, NX)
    sib = y * 2 + (1 - c)

    def at_y(step):
        return lax.rem(y + (step + NY), NY) * 2 + c

    def at_z(step):
        return lax.rem(z + (step + NZ), NZ)

    def at_x(step):
        return lax.rem(x + (step + NX), NX)

    def remote(src, dst, send, recv, to):
        return pltpu.make_async_remote_copy(
            src_ref=src,
            dst_ref=dst,
            send_sem=send,
            recv_sem=recv,
            device_id=to,
            device_id_type=MESH,
        )

    half = pl.ds(pl.multiple_of(c * H, 128), H)
    mine = [
        pltpu.make_async_copy(qkv.at[:, :, half], wall.at[pl.ds(0, 3), z, x], loc.at[0]),
        pltpu.make_async_copy(wo.at[:, half], wall.at[3, z, x], loc.at[1]),
        pltpu.make_async_copy(win, win_all.at[dp], loc.at[2]),
        pltpu.make_async_copy(wout, wout_all.at[dp], loc.at[3]),
    ]
    for copy in mine:
        copy.start()

    swap = remote(frames, pbuf, m_s.at[0], m_r.at[0], (at_y(2), ex))
    swap.start()

    def ring(count, base, view, step_at, device):
        last = count // 2

        def pair(step):
            r, l = step_at(-(step - 1)), step_at(step - 1)
            if step == last:
                right, left = view(r, 0, 2), view(l, 2, 2)
            else:
                right, left = view(r, 0, 4), view(l, 0, 4)
            i = base + 2 * (step - 1)
            return (
                remote(right, right, ring_s.at[i], ring_r.at[i], device(1)),
                remote(left, left, ring_s.at[i + 1], ring_r.at[i + 1], device(-1)),
            )

        def arrived(step):
            r, l = step_at(-step), step_at(step)
            if step == last:
                right, left = view(r, 0, 2), view(l, 2, 2)
            else:
                right, left = view(r, 0, 4), view(l, 0, 4)
            i = base + 2 * (step - 1)
            return (
                remote(right, right, ring_s.at[i], ring_r.at[i], device(1)),
                remote(left, left, ring_s.at[i + 1], ring_r.at[i + 1], device(-1)),
            )

        def begin(step):
            for copy in pair(step):
                copy.start()

        def wait(step):
            for copy in arrived(step):
                copy.wait_recv()

        def finish():
            for step in range(1, last + 1):
                for copy in pair(step):
                    copy.wait_send()

        return begin, wait, finish, last

    def to_x(step):
        return (dp, z * NX + at_x(step))

    def to_z(step):
        return (dp, at_z(step) * NX + x)

    x_small = ring(NX, 0, lambda k, a, n: wall.at[pl.ds(a, n), z, k], at_x, to_x)
    z_large = ring(NZ, 4, lambda k, a, n: wall.at[pl.ds(a, n), k], at_z, to_z)
    z_small = ring(NZ, 4, lambda k, a, n: wall.at[pl.ds(a, n), k, x], at_z, to_z)
    x_large = ring(NX, 0, lambda k, a, n: wall.at[pl.ds(a, n), :, k], at_x, to_x)

    mine[0].wait()
    mine[1].wait()

    @pl.when(c == 0)
    def _():
        x_small[0](1)

    @pl.when(c == 1)
    def _():
        z_small[0](1)

    def w_in(kind, block, to):
        return remote(win_all.at[block], win_all.at[block], w_s.at[kind], w_r.at[kind], (to, ex))

    def w_out(kind, block, to):
        return remote(wout_all.at[block], wout_all.at[block], w_s.at[kind], w_r.at[kind], (to, ex))

    right, left = at_y(1), at_y(-1)
    mine[2].wait()
    mine[3].wait()
    weights = [
        w_in(0, dp, right),
        w_out(3, dp, left),
        w_out(1, dp, right),
        w_in(2, dp, left),
        w_in(4, dp, sib),
        w_out(5, dp, sib),
    ]
    for copy in weights:
        copy.start()

    @pl.when(c == 0)
    def _():
        for step in range(1, x_small[3]):
            x_small[1](step)
            x_small[0](step + 1)
        x_small[1](x_small[3])
        z_large[0](1)

    @pl.when(c == 1)
    def _():
        for step in range(1, z_small[3]):
            z_small[1](step)
            z_small[0](step + 1)
        z_small[1](z_small[3])
        x_large[0](1)

    named = (ids_t[0:1, :] == iota((NE, F), 0)) | (ids_t[1:2, :] == iota((NE, F), 0))
    before = onehot(iota((F, F), 0) < iota((F, F), 1))
    rank = jnp.where(named, dot(onehot(named), before), -1.0).astype(BF)
    rows = NE * R
    spread = onehot(lax.div(iota((rows, NE), 0), R) == iota((rows, NE), 1))
    rank = dot(spread, rank)
    slot = iota((rows, F), 0)
    pick[...] = onehot(rank == lax.rem(slot, R).astype(F32))
    pick_x[...] = onehot(rank == (lax.rem(slot, 4) + R).astype(F32))

    swap.wait_recv()
    stay = keep[0:1, 0:1] > 0.5
    stream = jnp.where(stay, frames[...].astype(F32), pbuf[...].astype(F32))
    strm[...] = stream.astype(BF)
    normed[c] = layer_norm(stream, gains[0:1, :]).astype(BF)
    share = remote(normed.at[c], normed.at[c], m_s.at[1], m_r.at[1], (sib, ex))
    share.start()

    @pl.when(c == 0)
    def _():
        for step in range(1, z_large[3]):
            z_large[1](step)
            z_large[0](step + 1)
        z_large[1](z_large[3])
        x_small[2]()
        z_large[2]()

    @pl.when(c == 1)
    def _():
        for step in range(1, x_large[3]):
            x_large[1](step)
            x_large[0](step + 1)
        x_large[1](x_large[3])
        z_small[2]()
        x_large[2]()

    give_wo = remote(wall.at[3], wo_sib, m_s.at[2], m_r.at[2], (sib, ex))
    give_wo.start()
    remote(
        normed.at[1 - c], normed.at[1 - c], m_s.at[1], m_r.at[1], (sib, ex)
    ).wait_recv()

    @pl.loop(0, 3)
    def _(m):
        w = wall[m].reshape(D, H)
        for s in range(2):
            proj[m, s] = dot(normed[s], w).astype(BF)

    lane = iota((F, 128), 1)

    def attend(s, store):
        @pl.loop(0, H // 128)
        def _(h):
            cols = pl.ds(pl.multiple_of(h * 128, 128), 128)
            q = proj[0, s, :, cols] * jnp.asarray(HEAD_DIM**-0.5, BF)
            k = proj[1, s, :, cols]
            v = proj[2, s, :, cols]
            zero = jnp.zeros_like(q)
            for_both = jnp.concatenate(
                [jnp.where(lane < HEAD_DIM, q, zero), jnp.where(lane < HEAD_DIM, zero, q)], axis=0
            )
            scores = lax.dot_general(
                for_both, k, (((1,), (1,)), ((), ())), preferred_element_type=F32
            )
            scores = jnp.exp(scores - jnp.max(scores, axis=-1, keepdims=True))
            probs = (scores / jnp.sum(scores, axis=-1, keepdims=True)).astype(BF)
            both = dot(probs, v)
            store(cols, jnp.where(lane < HEAD_DIM, both[:F], both[F:]).astype(BF))

    def store_other(cols, value):
        ctxs[:, cols] = value

    def store_own(cols, value):
        ctxh[c, :, cols] = value

    attend(1 - c, store_other)
    give_ctx = remote(ctxs, ctxh.at[c], m_s.at[3], m_r.at[3], (sib, ex))
    give_ctx.start()
    attend(c, store_own)
    remote(wo_sib, wo_sib, m_s.at[2], m_r.at[2], (sib, ex)).wait_recv()
    remote(
        ctxh.at[1 - c], ctxh.at[1 - c], m_s.at[3], m_r.at[3], (sib, ex)
    ).wait_recv()

    def project(w):
        return dot(ctxh[0], w[:H]) + dot(ctxh[1], w[H:])

    other = pl.ds(pl.multiple_of((1 - c) * H, 128), H)
    mixed[:, half] = (strm[:, half].astype(F32) + project(wall[3].reshape(D, H))).astype(BF)
    mixed[:, other] = (strm[:, other].astype(F32) + project(wo_sib[...].reshape(D, H))).astype(BF)
    normed2 = layer_norm(mixed[...].astype(F32), gains[1:2, :]).astype(BF)

    tx[:, :, 0:D] = dot(pick[...], normed2).astype(BF).reshape(NE, R, D)
    tail = dot(pick_x[...], normed2)
    part = lax.div(lax.rem(iota((rows, X), 0), R), 4)
    packed = tail[:, 0:X]
    for p in range(1, 4):
        packed = jnp.where(part == p, tail[:, p * X : (p + 1) * X], packed)
    tx[:, :, D : D + X] = packed.astype(BF).reshape(NE, R, X)

    def away(k):
        return lax.rem(z + lax.div(k, NX), NZ) * NX + lax.rem(x + lax.rem(k, NX), NX)

    def back(k):
        return lax.rem(z + NZ - lax.div(k, NX), NZ) * NX + lax.rem(x + NX - lax.rem(k, NX), NX)

    def send_out(k):
        to = away(k)
        return remote(tx.at[to], rx.at[ex], t_s.at[k], t_r.at[k], (dp, to))

    def came_in(k):
        src = back(k)
        return remote(rx.at[src], rx.at[src], t_s.at[k], t_r.at[k], (dp, src))

    def give_back(k):
        to = back(k)
        return remote(ry.at[to], fx.at[ex], f_s.at[k], f_r.at[k], (dp, to))

    def got_back(k):
        src = away(k)
        return remote(fx.at[src], fx.at[src], f_s.at[k], f_r.at[k], (dp, src))

    @pl.loop(1, NE)
    def _(k):
        send_out(k).start()

    rx[ex] = tx[ex]

    r0 = router[...].astype(BF)
    r1 = (router[...] - r0.astype(F32)).astype(BF)
    r2 = (router[...] - r0.astype(F32) - r1.astype(F32)).astype(BF)
    logits = dot(normed2, r0) + (dot(normed2, r1) + dot(normed2, r2))
    expert = iota((F, NE), 1)
    first, second = ids[:, 0:1] == expert, ids[:, 1:2] == expert
    zero = jnp.zeros_like(logits)
    ahead = jnp.sum(jnp.where(first, logits, zero), axis=1, keepdims=True) - jnp.sum(
        jnp.where(second, logits, zero), axis=1, keepdims=True
    )
    gate = 1.0 / (1.0 + jnp.exp(-ahead))
    gates = jnp.where(first, gate, jnp.where(second, 1.0 - gate, zero))
    either = onehot(first | second)
    earlier = onehot(iota((F, F), 1) < iota((F, F), 0))
    rank_f = jnp.where(first | second, dot(earlier, either), -1.0).astype(BF)
    spread_f = onehot(lax.div(iota((NE, rows), 1), R) == iota((NE, rows), 0))
    rank_f = dot(rank_f, spread_f)
    gates_hi = gates.astype(BF)
    gates_lo = (gates - gates_hi.astype(F32)).astype(BF)
    gates_hi, gates_lo = dot(gates_hi, spread_f), dot(gates_lo, spread_f)
    slot_f = iota((F, rows), 1)

    def go_on(kind, make, block, to):
        copy = make(kind, block, to)
        copy.start()
        weights.append(copy)

    w_in(0, left, right).wait_recv()
    go_on(6, w_in, left, right)
    go_on(8, w_in, left, sib)
    w_out(3, right, left).wait_recv()
    go_on(7, w_out, right, left)
    go_on(9, w_out, right, sib)
    w_out(1, left, right).wait_recv()
    go_on(10, w_out, left, sib)
    w_in(2, right, left).wait_recv()
    go_on(11, w_in, right, sib)

    @pl.loop(1, NE)
    def _(k):
        came_in(k).wait_recv()

    xr[0:rows] = rx[:, :, 0:D].reshape(rows, D)
    extra = rx[:, :, D : D + X].reshape(rows, X)
    more = NE * 4

    def unpack(p):
        i, j = iota((more, rows), 1), iota((more, rows), 0)
        return onehot(
            (lax.div(i, R) == lax.div(j, 4)) & (lax.rem(i, R) == 4 * p + lax.rem(j, 4))
        )

    for p in range(4):
        xr[rows : rows + more, p * X : (p + 1) * X] = dot(unpack(p), extra).astype(BF)

    total = rows + more
    tile = total // 2

    def expert_slice(d, begin):
        @pl.loop(0, total // tile)
        def _(t):
            at = pl.ds(pl.multiple_of(t * tile, 16), tile)
            v = dot(xr[at], win_all[d])
            hidden = (0.5 * v * (1.0 + jnp.tanh(0.5 * v))).astype(BF)
            partial = dot(hidden, wout_all[d])
            if begin:
                acc[at] = partial
            else:
                acc[at] = acc[at] + partial

    far = at_y(2)

    def of_sib(d):
        return d + (1 - 2 * c)

    expert_slice(dp, True)
    w_in(4, sib, sib).wait_recv()
    w_out(5, sib, sib).wait_recv()
    expert_slice(sib, False)
    expert_slice(left, False)
    expert_slice(right, False)
    w_in(8, of_sib(left), sib).wait_recv()
    w_out(10, of_sib(left), sib).wait_recv()
    expert_slice(of_sib(left), False)
    w_in(11, of_sib(right), sib).wait_recv()
    w_out(9, of_sib(right), sib).wait_recv()
    expert_slice(of_sib(right), False)
    w_in(6, far, right).wait_recv()
    go_on(12, w_in, far, sib)
    w_out(7, far, left).wait_recv()
    go_on(13, w_out, far, sib)
    expert_slice(far, False)
    w_in(12, of_sib(far), sib).wait_recv()
    w_out(13, of_sib(far), sib).wait_recv()
    expert_slice(of_sib(far), False)

    ry[:, :, 0:D] = acc[0:rows].astype(BF).reshape(NE, R, D)
    packed = None
    for p in range(4):
        piece = lax.dot_general(
            unpack(p),
            acc[rows : rows + more, p * X : (p + 1) * X].astype(BF),
            (((0,), (0,)), ((), ())),
            preferred_element_type=F32,
        )
        packed = piece if packed is None else packed + piece
    ry[:, :, D : D + X] = packed.astype(BF).reshape(NE, R, X)

    @pl.loop(1, NE)
    def _(k):
        give_back(k).start()

    fx[ex] = ry[ex]
    in_place = rank_f == lax.rem(slot_f, R).astype(F32)
    in_tail = rank_f == (lax.rem(slot_f, 4) + R).astype(F32)
    quarter = lax.div(lax.rem(slot_f, R), 4)

    def on(mask, values):
        return jnp.where(mask, values, 0.0).astype(BF)

    main_hi, main_lo = on(in_place, gates_hi), on(in_place, gates_lo)

    @pl.loop(1, NE)
    def _(k):
        got_back(k).wait_recv()

    last = fx[:, :, D : D + X].reshape(rows, X)
    for p in range(4):
        cols = slice(p * X, (p + 1) * X)
        body = fx[:, :, cols].reshape(rows, X)
        here = in_tail & (quarter == p)
        out[:, cols] = (
            mixed[:, cols].astype(F32)
            + (dot(main_hi, body) + dot(on(here, gates_hi), last))
            + (dot(main_lo, body) + dot(on(here, gates_lo), last))
        ).astype(BF)

    @pl.loop(1, NE)
    def _(k):
        send_out(k).wait_send()
        give_back(k).wait_send()

    for copy in weights + [swap, share, give_wo, give_ctx]:
        copy.wait_send()


def body(
    frames_in, pit_order, expert_ids, norm_gains, attn_qkv, attn_out, router, expert_in, expert_out
):
    dp_index = lax.axis_index("dp")
    exp_index = lax.axis_index("expert")
    speaker = dp_index // (NY * 2 // 2)
    meeting = dp_index % NY * NE + exp_index
    keep = (pit_order[meeting, speaker] == speaker).astype(F32)
    keep = jnp.broadcast_to(keep, (8, 128))
    ids = expert_ids[0]
    vmem = pl.BlockSpec(memory_space=pltpu.VMEM)
    hbm = pl.BlockSpec(memory_space=pl.ANY)
    dma = pltpu.SemaphoreType.DMA
    rows = NE * R
    out = pl.pallas_call(
        kernel,
        out_shape=jax.ShapeDtypeStruct((F, D), BF),
        in_specs=[vmem] * 6 + [hbm] * 4,
        out_specs=vmem,
        scratch_shapes=[
            pltpu.VMEM((F, D), BF),
            pltpu.VMEM((F, D), BF),
            pltpu.VMEM((2, F, D), BF),
            pltpu.VMEM((4, NZ, NX, D // NE, H), BF),
            pltpu.VMEM((NZ, NX, D // NE, H), BF),
            pltpu.VMEM((3, 2, F, H), BF),
            pltpu.VMEM((2, F, H), BF),
            pltpu.VMEM((F, H), BF),
            pltpu.VMEM((F, D), BF),
            pltpu.VMEM((NE, R, D + X), BF),
            pltpu.VMEM((NE, R, D + X), BF),
            pltpu.VMEM((NE, R, D + X), BF),
            pltpu.VMEM((NE, R, D + X), BF),
            pltpu.VMEM((NE * CAP, D), BF),
            pltpu.VMEM((NE * CAP, D), F32),
            pltpu.VMEM((2 * NY, D, H), BF),
            pltpu.VMEM((2 * NY, H, D), BF),
            pltpu.VMEM((rows, F), BF),
            pltpu.VMEM((rows, F), BF),
            dma((12,)),
            dma((12,)),
            dma((14,)),
            dma((14,)),
            dma((4,)),
            dma((4,)),
            dma((NE,)),
            dma((NE,)),
            dma((NE,)),
            dma((NE,)),
            dma((4,)),
        ],
        compiler_params=pltpu.CompilerParams(
            has_side_effects=True, vmem_limit_bytes=60 * 2**20
        ),
        cost_estimate=pl.CostEstimate(
            flops=14 * 10**9, bytes_accessed=8 * 2**20, transcendentals=4 * 10**6
        ),
    )(
        keep,
        ids,
        ids.T,
        norm_gains,
        router,
        frames_in[0],
        attn_qkv,
        attn_out,
        expert_in[0],
        expert_out[0],
    )
    return out[None]


def solution(mesh):
    return jax.shard_map(
        body,
        mesh=mesh,
        in_specs=(
            P(("dp", "expert"), None, None),
            P(),
            P(("dp", "expert"), None, None),
            P(),
            P(None, "expert", None),
            P("expert", None),
            P(),
            P("expert", None, "dp"),
            P("expert", "dp", None),
        ),
        out_specs=P(("dp", "expert"), None, None),
        check_vma=False,
    )
```

time: 499 us -> 162 us (0.32)
  waiting for transfers between devices: 313 us -> 0 us
  Pallas kernels: 0 us -> 155 us
  local copies, waits for them, and re-layouts: 76.9 us -> 6.24 us
  blocking collectives: 39.2 us -> 0 us
  matrix products: 31.9 us -> 0 us
  starting transfers between devices: 13.8 us -> 0 us
  between operations: 14.1 us -> 0.67 us
    all_gather x3 -> x0, waiting for transfers between devices: 203 us -> none  [the longest x1 78.7 us: body(): lax.all_gather(attn_qkv, 'expert', axis=1, tiled=True)]
    pallas_call x0 -> x1, Pallas kernels: none -> 155 us  [body(): pl.pallas_call(kernel, out_shape=jax.ShapeDtypeStruct((F, D), BF), in_spe...]
    reduce_scatter x1 -> x0, waiting for transfers between devices: 74.4 us -> none  [body(): lax.psum_scatter(partials, 'dp', scatter_dimension=0, tiled=True)]
    all_to_all x1 -> x0, blocking collectives: 39.2 us -> none  [body(): lax.all_to_all(outgoing, 'expert', split_axis=0, concat_axis=0, tiled=True)]
    reshape x5 -> x0, local copies, waits for them, and re-layouts: 38.6 us -> none  [the longest x1 16.5 us: body(): flat_rows = piece.reshape(-1, piece.shape[-1])]
    all_to_all x1 -> x0, waiting for transfers between devices: 30.1 us -> none  [body(): lax.all_to_all(answer, 'expert', split_axis=0, concat_axis=0, tiled=True)]
    dot_general x5 -> x0, matrix products: 27.4 us -> none  [the longest x1 17.1 us: body(): jnp.dot(hidden, expert_out[0], preferred_element_type=jnp.float32)]
    all_gather x1 -> x0, local copies, waits for them, and re-layouts: 14.1 us -> none  [body(): lax.all_gather(lax.all_to_all(outgoing, 'expert', split_axis=0, concat_ax...]
  transfers between devices with their start and end apart: 6 -> 0, of which waited for: 6 -> 0; matrix products, arithmetic and copies ran while one was open for 5% -> 0% of each run, Pallas kernels for 0% -> 0%
where the time goes in v1:
time: 162 us
  Pallas kernels  155 us (96%)
  local copies, waits for them, and re-layouts  6.24 us (4%)
    pallas_call x1, Pallas kernels, body(): pl.pallas_call(kernel, out_shape=jax.ShapeDtypeStruct((F, D), BF), in_spe...  155 us

profile of v1, /device:TPU:1, one launch (start us, length us, event | category | flops | bytes accessed | tf_op | source)
XLA Modules:
  0.0 161.7 jit_solution(15653341795251006020)
XLA Ops:
  0.0 0.0 copy-start
  0.0 1.3 dynamic_slice.3
  2.0 0.6 broadcast_in_dim.6.keep
  2.5 1.5 copy.10.ids
  4.0 0.0 copy-done
  4.0 1.0 copy.11.router
  5.0 154.8 %shard_map.91 = bf16[256,1024]{1,0:T(8,128)(2,1)} custom-call(f32[8,128]{1,0:T(8,128)} %broadcast_in_dim.6.keep, s32[256,2]{1,0:T(8,128)} %copy.10.ids, s32[2,256]{1,0:T(2,128)} %bitcast.10, f32[2,1024]{1,0:T(2,128)} %gains.1, f32[1024,32]{1,0:T(8,128)} %copy.11.router, bf16[256,1024]{1,0:T(8,128)(2,1)} %bitcast.13, bf16[3,32,1024]{2,1,0:T(8,128)(2,1)} %qkv.1, ...), custom_call_target="tpu_custom_call" | custom-call | flops 14000000000 | bytes 8388608 | tf_op jit(solution)/shard_map/pallas_call | solution.py:512
  159.8 1.9 %copy.13 = bf16[1,256,1024]{2,1,0:T(8,128)(2,1)} copy(bf16[1,256,1024]{2,1,0:T(8,128)(2,1)} %bitcast.8) | data formatting | bytes 1048576
Async XLA Ops:
  0.0 4.0 %copy-start = (f32[1024,32]{0,1:T(8,128)S(1)}, f32[1024,32]{0,1:T(8,128)}, u32[]{:S(2)}) copy-start(f32[1024,32]{0,1:T(8,128)} %param.15) | copy-start | bytes 393220

commit v2 on v1

--- a/solution.py
+++ b/solution.py
@@ -1,3 +1,5 @@
+import functools
+
 import jax
 import jax.numpy as jnp
 from jax import lax
@@ -18,6 +20,7 @@
 R = 16
 CAP = 20
 X = 256
+MEETINGS = 128
 epsilon = 1e-05
 
 
@@ -41,8 +44,7 @@
 
 
 def kernel(
-    keep,
-    ids,
+    order,
     ids_t,
     gains,
     router,
@@ -108,6 +110,18 @@
             device_id_type=MESH,
         )
 
+    barrier = pltpu.get_barrier_semaphore()
+
+    def greet(to):
+        pl.semaphore_signal(barrier, inc=1, device_id=to, device_id_type=MESH)
+
+    for to in (at_y(1), at_y(-1), at_y(2), sib):
+        greet((to, ex))
+
+    @pl.loop(1, NE)
+    def _(k):
+        greet((dp, lax.rem(ex + k, NE)))
+
     half = pl.ds(pl.multiple_of(c * H, 128), H)
     mine = [
         pltpu.make_async_copy(qkv.at[:, :, half], wall.at[pl.ds(0, 3), z, x], loc.at[0]),
@@ -117,51 +131,43 @@
     ]
     for copy in mine:
         copy.start()
+    pl.semaphore_wait(barrier, NE - 1 + 4)
 
     swap = remote(frames, pbuf, m_s.at[0], m_r.at[0], (at_y(2), ex))
     swap.start()
 
-    def ring(count, base, view, step_at, device):
-        last = count // 2
-
-        def pair(step):
-            r, l = step_at(-(step - 1)), step_at(step - 1)
-            if step == last:
-                right, left = view(r, 0, 2), view(l, 2, 2)
-            else:
-                right, left = view(r, 0, 4), view(l, 0, 4)
-            i = base + 2 * (step - 1)
+    class Ring:
+        def __init__(self, count, base, view, step_at, device):
+            self.last = count // 2
+            self.base, self.view, self.step_at, self.device = base, view, step_at, device
+
+        def pair(self, step, hop):
+            last = step == self.last
+            right = self.view(self.step_at(hop - step), pl.ds(0, H // 2 if last else H))
+            left = self.view(self.step_at(step - hop), pl.ds(H // 2 if last else 0, H // 2 if last else H))
+            i = self.base + 2 * (step - 1)
             return (
-                remote(right, right, ring_s.at[i], ring_r.at[i], device(1)),
-                remote(left, left, ring_s.at[i + 1], ring_r.at[i + 1], device(-1)),
+                remote(right, right, ring_s.at[i], ring_r.at[i], self.device(1)),
+                remote(left, left, ring_s.at[i + 1], ring_r.at[i + 1], self.device(-1)),
             )
 
-        def arrived(step):
-            r, l = step_at(-step), step_at(step)
-            if step == last:
-                right, left = view(r, 0, 2), view(l, 2, 2)
-            else:
-                right, left = view(r, 0, 4), view(l, 0, 4)
-            i = base + 2 * (step - 1)
-            return (
-                remote(right, right, ring_s.at[i], ring_r.at[i], device(1)),
-                remote(left, left, ring_s.at[i + 1], ring_r.at[i + 1], device(-1)),
-            )
-
-        def begin(step):
-            for copy in pair(step):
+        def begin(self, step):
+            for copy in self.pair(step, 1):
                 copy.start()
 
-        def wait(step):
-            for copy in arrived(step):
+        def wait(self, step):
+            for copy in self.pair(step, 0):
                 copy.wait_recv()
 
-        def finish():
-            for step in range(1, last + 1):
-                for copy in pair(step):
+        def relay(self, step):
+            self.wait(step)
+            if step < self.last:
+                self.begin(step + 1)
+
+        def finish(self):
+            for step in range(1, self.last + 1):
+                for copy in self.pair(step, 1):
                     copy.wait_send()
-
-        return begin, wait, finish, last
 
     def to_x(step):
         return (dp, z * NX + at_x(step))
@@ -169,21 +175,40 @@
     def to_z(step):
         return (dp, at_z(step) * NX + x)
 
-    x_small = ring(NX, 0, lambda k, a, n: wall.at[pl.ds(a, n), z, k], at_x, to_x)
-    z_large = ring(NZ, 4, lambda k, a, n: wall.at[pl.ds(a, n), k], at_z, to_z)
-    z_small = ring(NZ, 4, lambda k, a, n: wall.at[pl.ds(a, n), k, x], at_z, to_z)
-    x_large = ring(NX, 0, lambda k, a, n: wall.at[pl.ds(a, n), :, k], at_x, to_x)
+    chunks = ((0, 2), (2, 1), (3, 1))
+    small, large = {0: [], 1: []}, {0: [], 1: []}
+    for i, (m, n) in enumerate(chunks):
+        mats = pl.ds(m, n)
+        bx, bz = 12 * i, 12 * i + 4
+        small[0].append(Ring(NX, bx, lambda k, w, mats=mats: wall.at[mats, z, k, :, w], at_x, to_x))
+        large[0].append(Ring(NZ, bz, lambda k, w, mats=mats: wall.at[mats, k, :, :, w], at_z, to_z))
+        small[1].append(Ring(NZ, bz, lambda k, w, mats=mats: wall.at[mats, k, x, :, w], at_z, to_z))
+        large[1].append(Ring(NX, bx, lambda k, w, mats=mats: wall.at[mats, :, k, :, w], at_x, to_x))
 
     mine[0].wait()
     mine[1].wait()
 
-    @pl.when(c == 0)
-    def _():
-        x_small[0](1)
-
-    @pl.when(c == 1)
-    def _():
-        z_small[0](1)
+    def on_core(core, work):
+        pl.when(c == core)(functools.partial(work, small[core], large[core]))
+
+    def start_small(small, large):
+        for ring in small:
+            ring.begin(1)
+
+    on_core(0, start_small)
+    on_core(1, start_small)
+
+    def small_to_large(small, large):
+        for step in range(1, small[0].last):
+            for ring in small:
+                ring.relay(step)
+        for near, wide in zip(small, large):
+            near.wait(near.last)
+            if wide is not large[-1]:
+                wide.begin(1)
+
+    on_core(0, small_to_large)
+    on_core(1, small_to_large)
 
     def w_in(kind, block, to):
         return remote(win_all.at[block], win_all.at[block], w_s.at[kind], w_r.at[kind], (to, ex))
@@ -205,22 +230,6 @@
     for copy in weights:
         copy.start()
 
-    @pl.when(c == 0)
-    def _():
-        for step in range(1, x_small[3]):
-            x_small[1](step)
-            x_small[0](step + 1)
-        x_small[1](x_small[3])
-        z_large[0](1)
-
-    @pl.when(c == 1)
-    def _():
-        for step in range(1, z_small[3]):
-            z_small[1](step)
-            z_small[0](step + 1)
-        z_small[1](z_small[3])
-        x_large[0](1)
-
     named = (ids_t[0:1, :] == iota((NE, F), 0)) | (ids_t[1:2, :] == iota((NE, F), 0))
     before = onehot(iota((F, F), 0) < iota((F, F), 1))
     rank = jnp.where(named, dot(onehot(named), before), -1.0).astype(BF)
@@ -232,42 +241,49 @@
     pick_x[...] = onehot(rank == (lax.rem(slot, 4) + R).astype(F32))
 
     swap.wait_recv()
-    stay = keep[0:1, 0:1] > 0.5
+    speaker = lax.div(y, NY // 2)
+    meeting = lax.rem(dp, NY) * NE + ex
+    here = (iota((2, MEETINGS), 0) == speaker) & (iota((2, MEETINGS), 1) == meeting)
+    source = jnp.sum(jnp.where(here, order[...], 0).astype(F32), axis=(0, 1), keepdims=True)
+    stay = source == speaker.astype(F32)
     stream = jnp.where(stay, frames[...].astype(F32), pbuf[...].astype(F32))
     strm[...] = stream.astype(BF)
     normed[c] = layer_norm(stream, gains[0:1, :]).astype(BF)
     share = remote(normed.at[c], normed.at[c], m_s.at[1], m_r.at[1], (sib, ex))
     share.start()
 
-    @pl.when(c == 0)
-    def _():
-        for step in range(1, z_large[3]):
-            z_large[1](step)
-            z_large[0](step + 1)
-        z_large[1](z_large[3])
-        x_small[2]()
-        z_large[2]()
-
-    @pl.when(c == 1)
-    def _():
-        for step in range(1, x_large[3]):
-            x_large[1](step)
-            x_large[0](step + 1)
-        x_large[1](x_large[3])
-        z_small[2]()
-        x_large[2]()
-
-    give_wo = remote(wall.at[3], wo_sib, m_s.at[2], m_r.at[2], (sib, ex))
-    give_wo.start()
+    def most(small, large):
+        for step in range(1, large[0].last):
+            for ring in large[:2]:
+                ring.relay(step)
+        large[0].wait(large[0].last)
+        large[2].begin(1)
+
+    def values(small, large):
+        large[1].wait(large[1].last)
+
+    def output(step, small, large):
+        if step <= large[2].last:
+            large[2].relay(step)
+
+    def go_round(step):
+        on_core(0, functools.partial(output, step))
+        on_core(1, functools.partial(output, step))
+
+    on_core(0, most)
+    on_core(1, most)
     remote(
         normed.at[1 - c], normed.at[1 - c], m_s.at[1], m_r.at[1], (sib, ex)
     ).wait_recv()
 
-    @pl.loop(0, 3)
-    def _(m):
+    for m in range(3):
+        if m == 2:
+            on_core(0, values)
+            on_core(1, values)
         w = wall[m].reshape(D, H)
         for s in range(2):
             proj[m, s] = dot(normed[s], w).astype(BF)
+        go_round(m + 1)
 
     lane = iota((F, 128), 1)
 
@@ -297,6 +313,9 @@
         ctxh[c, :, cols] = value
 
     attend(1 - c, store_other)
+    go_round(4)
+    give_wo = remote(wall.at[3], wo_sib, m_s.at[2], m_r.at[2], (sib, ex))
+    give_wo.start()
     give_ctx = remote(ctxs, ctxh.at[c], m_s.at[3], m_r.at[3], (sib, ex))
     give_ctx.start()
     attend(c, store_own)
@@ -352,9 +371,15 @@
     r0 = router[...].astype(BF)
     r1 = (router[...] - r0.astype(F32)).astype(BF)
     r2 = (router[...] - r0.astype(F32) - r1.astype(F32)).astype(BF)
-    logits = dot(normed2, r0) + (dot(normed2, r1) + dot(normed2, r2))
+
+    def along(b):
+        return lax.dot_general(normed2, b, (((1,), (1,)), ((), ())), preferred_element_type=F32)
+
+    logits = along(r0) + (along(r1) + along(r2))
     expert = iota((F, NE), 1)
-    first, second = ids[:, 0:1] == expert, ids[:, 1:2] == expert
+    chosen = jnp.concatenate([ids_t[...], jnp.zeros((6, F), jnp.int32)], axis=0).astype(F32).T
+    chosen = chosen.astype(jnp.int32)
+    first, second = chosen[:, 0:1] == expert, chosen[:, 1:2] == expert
     zero = jnp.zeros_like(logits)
     ahead = jnp.sum(jnp.where(first, logits, zero), axis=1, keepdims=True) - jnp.sum(
         jnp.where(second, logits, zero), axis=1, keepdims=True
@@ -494,17 +519,17 @@
     for copy in weights + [swap, share, give_wo, give_ctx]:
         copy.wait_send()
 
+    def finish(small, large):
+        for ring in small + large:
+            ring.finish()
+
+    on_core(0, finish)
+    on_core(1, finish)
+
 
 def body(
     frames_in, pit_order, expert_ids, norm_gains, attn_qkv, attn_out, router, expert_in, expert_out
 ):
-    dp_index = lax.axis_index("dp")
-    exp_index = lax.axis_index("expert")
-    speaker = dp_index // (NY * 2 // 2)
-    meeting = dp_index % NY * NE + exp_index
-    keep = (pit_order[meeting, speaker] == speaker).astype(F32)
-    keep = jnp.broadcast_to(keep, (8, 128))
-    ids = expert_ids[0]
     vmem = pl.BlockSpec(memory_space=pltpu.VMEM)
     hbm = pl.BlockSpec(memory_space=pl.ANY)
     dma = pltpu.SemaphoreType.DMA
@@ -512,7 +537,7 @@
     out = pl.pallas_call(
         kernel,
         out_shape=jax.ShapeDtypeStruct((F, D), BF),
-        in_specs=[vmem] * 6 + [hbm] * 4,
+        in_specs=[vmem] * 5 + [hbm] * 4,
         out_specs=vmem,
         scratch_shapes=[
             pltpu.VMEM((F, D), BF),
@@ -534,8 +559,8 @@
             pltpu.VMEM((2 * NY, H, D), BF),
             pltpu.VMEM((rows, F), BF),
             pltpu.VMEM((rows, F), BF),
-            dma((12,)),
-            dma((12,)),
+            dma((36,)),
+            dma((36,)),
             dma((14,)),
             dma((14,)),
             dma((4,)),
@@ -547,17 +572,16 @@
             dma((4,)),
         ],
         compiler_params=pltpu.CompilerParams(
-            has_side_effects=True, vmem_limit_bytes=60 * 2**20
+            collective_id=0, has_side_effects=True, vmem_limit_bytes=60 * 2**20
         ),
         cost_estimate=pl.CostEstimate(
             flops=14 * 10**9, bytes_accessed=8 * 2**20, transcendentals=4 * 10**6
         ),
     )(
-        keep,
-        ids,
-        ids.T,
+        pit_order.T,
+        expert_ids[0].T,
         norm_gains,
-        router,
+        router.T,
         frames_in[0],
         attn_qkv,
         attn_out,

time: 162 us -> 156 us (0.963)
  local copies, waits for them, and re-layouts: 6.24 us -> 1.87 us
where the time goes in v2:
time: 156 us
  Pallas kernels  154 us (99%)
  local copies, waits for them, and re-layouts  1.87 us (1%)
    pallas_call x1, Pallas kernels, body(): pl.pallas_call(kernel, out_shape=jax.ShapeDtypeStruct((F, D), BF), in_spe...  154 us

profile of v2, /device:TPU:1, one launch (start us, length us, event | category | flops | bytes accessed | tf_op | source)
XLA Modules:
  0.0 155.6 jit_solution(4344500332887096215)
XLA Ops:
  0.0 153.7 %shard_map.91 = bf16[256,1024]{1,0:T(8,128)(2,1)} custom-call(s32[2,128]{1,0:T(2,128)} %bitcast.15, s32[2,256]{1,0:T(2,128)} %bitcast.14, f32[2,1024]{1,0:T(2,128)} %gains.1, f32[32,1024]{1,0:T(8,128)} %bitcast.13, bf16[256,1024]{1,0:T(8,128)(2,1)} %bitcast.12, bf16[3,32,1024]{2,1,0:T(8,128)(2,1)} %qkv.1, bf16[32,1024]{1,0:T(8,128)(2,1)} %wo.1, ...), custom_call_target="tpu_custom_call" | custom-call | flops 14000000000 | bytes 8388608 | tf_op jit(solution)/shard_map/pallas_call | solution.py:537
  153.7 1.9 %copy.11 = bf16[1,256,1024]{2,1,0:T(8,128)(2,1)} copy(bf16[1,256,1024]{2,1,0:T(8,128)(2,1)} %bitcast.9) | data formatting | bytes 1048576

commit v3 on v2

--- a/solution.py
+++ b/solution.py
@@ -68,9 +68,11 @@
     ry,
     fx,
     xr,
+    hidden,
     acc,
     win_all,
     wout_all,
+    weigh,
     pick,
     pick_x,
     ring_s,
@@ -127,7 +129,8 @@
         pltpu.make_async_copy(qkv.at[:, :, half], wall.at[pl.ds(0, 3), z, x], loc.at[0]),
         pltpu.make_async_copy(wo.at[:, half], wall.at[3, z, x], loc.at[1]),
         pltpu.make_async_copy(win, win_all.at[dp], loc.at[2]),
-        pltpu.make_async_copy(wout, wout_all.at[dp], loc.at[3]),
+        pltpu.make_async_copy(wout.at[:, pl.ds(0, H)], wout_all.at[0, dp], loc.at[3]),
+        pltpu.make_async_copy(wout.at[:, pl.ds(H, H)], wout_all.at[1, dp], loc.at[4]),
     ]
     for copy in mine:
         copy.start()
@@ -175,7 +178,7 @@
     def to_z(step):
         return (dp, at_z(step) * NX + x)
 
-    chunks = ((0, 2), (2, 1), (3, 1))
+    chunks = ((0, 1), (1, 1), (2, 1), (3, 1))
     small, large = {0: [], 1: []}, {0: [], 1: []}
     for i, (m, n) in enumerate(chunks):
         mats = pl.ds(m, n)
@@ -197,38 +200,6 @@
 
     on_core(0, start_small)
     on_core(1, start_small)
-
-    def small_to_large(small, large):
-        for step in range(1, small[0].last):
-            for ring in small:
-                ring.relay(step)
-        for near, wide in zip(small, large):
-            near.wait(near.last)
-            if wide is not large[-1]:
-                wide.begin(1)
-
-    on_core(0, small_to_large)
-    on_core(1, small_to_large)
-
-    def w_in(kind, block, to):
-        return remote(win_all.at[block], win_all.at[block], w_s.at[kind], w_r.at[kind], (to, ex))
-
-    def w_out(kind, block, to):
-        return remote(wout_all.at[block], wout_all.at[block], w_s.at[kind], w_r.at[kind], (to, ex))
-
-    right, left = at_y(1), at_y(-1)
-    mine[2].wait()
-    mine[3].wait()
-    weights = [
-        w_in(0, dp, right),
-        w_out(3, dp, left),
-        w_out(1, dp, right),
-        w_in(2, dp, left),
-        w_in(4, dp, sib),
-        w_out(5, dp, sib),
-    ]
-    for copy in weights:
-        copy.start()
 
     named = (ids_t[0:1, :] == iota((NE, F), 0)) | (ids_t[1:2, :] == iota((NE, F), 0))
     before = onehot(iota((F, F), 0) < iota((F, F), 1))
@@ -239,6 +210,91 @@
     slot = iota((rows, F), 0)
     pick[...] = onehot(rank == lax.rem(slot, R).astype(F32))
     pick_x[...] = onehot(rank == (lax.rem(slot, 4) + R).astype(F32))
+
+    def small_to_large(small, large):
+        for step in range(1, small[0].last):
+            for ring in small:
+                ring.relay(step)
+        for near, wide in zip(small, large):
+            near.wait(near.last)
+            if wide is not large[-1]:
+                wide.begin(1)
+
+    on_core(0, small_to_large)
+    on_core(1, small_to_large)
+
+    right, left, far = at_y(1), at_y(-1), at_y(2)
+
+    def of_sib(d):
+        return d + (1 - 2 * c)
+
+    sent = []
+
+    class Chunk:
+        def __init__(self, base, ref, depth):
+            self.base, self.ref, self.depth = base, ref, depth
+
+        def copy(self, kind, d, to):
+            first = kind in (3, 7)
+            rows = pl.ds(0 if first or kind not in (4, 8) else self.depth // 2, self.depth // 2 if kind in (3, 4, 7, 8) else self.depth)
+            ref = self.ref.at[d, rows]
+            i = self.base + kind
+            return remote(ref, ref, w_s.at[i], w_r.at[i], (to, ex))
+
+        def send(self, kind, d, to):
+            copy = self.copy(kind, d, to)
+            copy.start()
+            sent.append(copy)
+
+        def wait(self, kind, d):
+            self.copy(kind, d, sib).wait_recv()
+
+        def own(self):
+            self.send(0, dp, right)
+            self.send(1, dp, left)
+            self.send(2, dp, sib)
+
+        def relay(self):
+            self.wait(0, left)
+            self.send(3, left, right)
+            self.send(5, left, sib)
+            self.wait(1, right)
+            self.send(4, right, left)
+            self.send(6, right, sib)
+
+        def relay_far(self):
+            self.wait(3, far)
+            self.send(7, far, sib)
+            self.wait(4, far)
+            self.send(8, far, sib)
+
+        def from_sib(self):
+            self.wait(2, sib)
+            self.wait(5, of_sib(left))
+            self.wait(6, of_sib(right))
+
+        def far_from_sib(self):
+            self.wait(7, of_sib(far))
+            self.wait(8, of_sib(far))
+
+    chunk_in = Chunk(0, win_all, D)
+    chunk_out = [Chunk(9 * (1 + h), wout_all.at[h], H) for h in range(2)]
+    for copy in mine[2:]:
+        copy.wait()
+    chunk_in.own()
+
+    def most(small, large):
+        steps = large[0].last
+        for step in range(1, min(3, steps)):
+            for ring in large[:3]:
+                ring.relay(step)
+            if step == 1:
+                large[3].begin(1)
+            else:
+                large[3].relay(step - 1)
+
+    on_core(0, most)
+    on_core(1, most)
 
     swap.wait_recv()
     speaker = lax.div(y, NY // 2)
@@ -252,38 +308,36 @@
     share = remote(normed.at[c], normed.at[c], m_s.at[1], m_r.at[1], (sib, ex))
     share.start()
 
-    def most(small, large):
-        for step in range(1, large[0].last):
-            for ring in large[:2]:
+    def rest(small, large):
+        for step in range(3, large[0].last):
+            for ring in large[:3]:
                 ring.relay(step)
-        large[0].wait(large[0].last)
-        large[2].begin(1)
-
-    def values(small, large):
-        large[1].wait(large[1].last)
-
-    def output(step, small, large):
-        if step <= large[2].last:
-            large[2].relay(step)
-
-    def go_round(step):
-        on_core(0, functools.partial(output, step))
-        on_core(1, functools.partial(output, step))
-
-    on_core(0, most)
-    on_core(1, most)
+            large[3].relay(step - 1)
+
+    def come(m, small, large):
+        large[m].wait(large[m].last)
+
+    def output(steps, small, large):
+        step = steps[0] if large[3].last == NZ // 2 else steps[1]
+        large[3].relay(step)
+
+    def on_both(work):
+        on_core(0, work)
+        on_core(1, work)
+
+    on_both(rest)
     remote(
         normed.at[1 - c], normed.at[1 - c], m_s.at[1], m_r.at[1], (sib, ex)
     ).wait_recv()
+    chunk_out[0].own()
 
     for m in range(3):
-        if m == 2:
-            on_core(0, values)
-            on_core(1, values)
+        on_both(functools.partial(come, m))
         w = wall[m].reshape(D, H)
         for s in range(2):
             proj[m, s] = dot(normed[s], w).astype(BF)
-        go_round(m + 1)
+        if m == 1:
+            on_both(functools.partial(output, (3, 1)))
 
     lane = iota((F, 128), 1)
 
@@ -313,7 +367,7 @@
         ctxh[c, :, cols] = value
 
     attend(1 - c, store_other)
-    go_round(4)
+    on_both(functools.partial(output, (4, 2)))
     give_wo = remote(wall.at[3], wo_sib, m_s.at[2], m_r.at[2], (sib, ex))
     give_wo.start()
     give_ctx = remote(ctxs, ctxh.at[c], m_s.at[3], m_r.at[3], (sib, ex))
@@ -340,33 +394,35 @@
         packed = jnp.where(part == p, tail[:, p * X : (p + 1) * X], packed)
     tx[:, :, D : D + X] = packed.astype(BF).reshape(NE, R, X)
 
+    def in_z(k):
+        i = lax.div(k, NX)
+        j, odd = lax.div(i, 2), lax.rem(i, 2)
+        return (1 - odd) * lax.rem(NZ // 2 - j, NZ // 2) + odd * (NZ // 2 + j)
+
     def away(k):
-        return lax.rem(z + lax.div(k, NX), NZ) * NX + lax.rem(x + lax.rem(k, NX), NX)
+        return lax.rem(z + in_z(k), NZ) * NX + lax.rem(x + lax.rem(k, NX), NX)
 
     def back(k):
-        return lax.rem(z + NZ - lax.div(k, NX), NZ) * NX + lax.rem(x + NX - lax.rem(k, NX), NX)
+        return lax.rem(z + NZ - in_z(k), NZ) * NX + lax.rem(x + NX - lax.rem(k, NX), NX)
 
     def send_out(k):
         to = away(k)
-        return remote(tx.at[to], rx.at[ex], t_s.at[k], t_r.at[k], (dp, to))
-
-    def came_in(k):
-        src = back(k)
-        return remote(rx.at[src], rx.at[src], t_s.at[k], t_r.at[k], (dp, src))
-
-    def give_back(k):
+        return remote(tx.at[to], rx.at[k], t_s.at[k], t_r.at[k], (dp, to))
+
+    def give_back(k, h):
         to = back(k)
-        return remote(ry.at[to], fx.at[ex], f_s.at[k], f_r.at[k], (dp, to))
-
-    def got_back(k):
+        return remote(ry.at[h, k], fx.at[h, ex], f_s.at[h * NE + k], f_r.at[h * NE + k], (dp, to))
+
+    def got_back(k, h):
         src = away(k)
-        return remote(fx.at[src], fx.at[src], f_s.at[k], f_r.at[k], (dp, src))
+        at = fx.at[h, src]
+        return remote(at, at, f_s.at[h * NE + k], f_r.at[h * NE + k], (dp, src))
 
     @pl.loop(1, NE)
     def _(k):
         send_out(k).start()
 
-    rx[ex] = tx[ex]
+    rx[0] = tx[ex]
 
     r0 = router[...].astype(BF)
     r1 = (router[...] - r0.astype(F32)).astype(BF)
@@ -396,127 +452,135 @@
     gates_hi, gates_lo = dot(gates_hi, spread_f), dot(gates_lo, spread_f)
     slot_f = iota((F, rows), 1)
 
-    def go_on(kind, make, block, to):
-        copy = make(kind, block, to)
-        copy.start()
-        weights.append(copy)
-
-    w_in(0, left, right).wait_recv()
-    go_on(6, w_in, left, right)
-    go_on(8, w_in, left, sib)
-    w_out(3, right, left).wait_recv()
-    go_on(7, w_out, right, left)
-    go_on(9, w_out, right, sib)
-    w_out(1, left, right).wait_recv()
-    go_on(10, w_out, left, sib)
-    w_in(2, right, left).wait_recv()
-    go_on(11, w_in, right, sib)
-
-    @pl.loop(1, NE)
-    def _(k):
-        came_in(k).wait_recv()
-
-    xr[0:rows] = rx[:, :, 0:D].reshape(rows, D)
-    extra = rx[:, :, D : D + X].reshape(rows, X)
-    more = NE * 4
+    in_place = rank_f == lax.rem(slot_f, R).astype(F32)
+    in_tail = rank_f == (lax.rem(slot_f, 4) + R).astype(F32)
+
+    def on(mask, values):
+        return jnp.where(mask, values, 0.0).astype(BF)
+
+    quarter = lax.div(lax.rem(slot_f, R), 4)
+    weigh[0] = on(in_place, gates_hi)
+    weigh[1] = on(in_place, gates_lo)
+    for p in range(4):
+        here = in_tail & (quarter == p)
+        weigh[2 + 2 * p] = on(here, gates_hi)
+        weigh[3 + 2 * p] = on(here, gates_lo)
+
+    chunk_in.relay()
+    chunk_out[1].own()
+
+    peers = NE // 2
+    whole, more = peers * R, peers * 4
+    group = whole + more
 
     def unpack(p):
-        i, j = iota((more, rows), 1), iota((more, rows), 0)
+        i, j = iota((more, whole), 1), iota((more, whole), 0)
         return onehot(
             (lax.div(i, R) == lax.div(j, 4)) & (lax.rem(i, R) == 4 * p + lax.rem(j, 4))
         )
 
-    for p in range(4):
-        xr[rows : rows + more, p * X : (p + 1) * X] = dot(unpack(p), extra).astype(BF)
-
-    total = rows + more
-    tile = total // 2
-
-    def expert_slice(d, begin):
-        @pl.loop(0, total // tile)
-        def _(t):
-            at = pl.ds(pl.multiple_of(t * tile, 16), tile)
-            v = dot(xr[at], win_all[d])
-            hidden = (0.5 * v * (1.0 + jnp.tanh(0.5 * v))).astype(BF)
-            partial = dot(hidden, wout_all[d])
-            if begin:
-                acc[at] = partial
-            else:
-                acc[at] = acc[at] + partial
-
-    far = at_y(2)
-
-    def of_sib(d):
-        return d + (1 - 2 * c)
-
-    expert_slice(dp, True)
-    w_in(4, sib, sib).wait_recv()
-    w_out(5, sib, sib).wait_recv()
-    expert_slice(sib, False)
-    expert_slice(left, False)
-    expert_slice(right, False)
-    w_in(8, of_sib(left), sib).wait_recv()
-    w_out(10, of_sib(left), sib).wait_recv()
-    expert_slice(of_sib(left), False)
-    w_in(11, of_sib(right), sib).wait_recv()
-    w_out(9, of_sib(right), sib).wait_recv()
-    expert_slice(of_sib(right), False)
-    w_in(6, far, right).wait_recv()
-    go_on(12, w_in, far, sib)
-    w_out(7, far, left).wait_recv()
-    go_on(13, w_out, far, sib)
-    expert_slice(far, False)
-    w_in(12, of_sib(far), sib).wait_recv()
-    w_out(13, of_sib(far), sib).wait_recv()
-    expert_slice(of_sib(far), False)
-
-    ry[:, :, 0:D] = acc[0:rows].astype(BF).reshape(NE, R, D)
-    packed = None
-    for p in range(4):
-        piece = lax.dot_general(
-            unpack(p),
-            acc[rows : rows + more, p * X : (p + 1) * X].astype(BF),
-            (((0,), (0,)), ((), ())),
-            preferred_element_type=F32,
-        )
-        packed = piece if packed is None else packed + piece
-    ry[:, :, D : D + X] = packed.astype(BF).reshape(NE, R, X)
-
-    @pl.loop(1, NE)
-    def _(k):
-        give_back(k).start()
-
-    fx[ex] = ry[ex]
-    in_place = rank_f == lax.rem(slot_f, R).astype(F32)
-    in_tail = rank_f == (lax.rem(slot_f, 4) + R).astype(F32)
-    quarter = lax.div(lax.rem(slot_f, R), 4)
-
-    def on(mask, values):
-        return jnp.where(mask, values, 0.0).astype(BF)
-
-    main_hi, main_lo = on(in_place, gates_hi), on(in_place, gates_lo)
-
-    @pl.loop(1, NE)
-    def _(k):
-        got_back(k).wait_recv()
-
-    last = fx[:, :, D : D + X].reshape(rows, X)
-    for p in range(4):
-        cols = slice(p * X, (p + 1) * X)
-        body = fx[:, :, cols].reshape(rows, X)
-        here = in_tail & (quarter == p)
-        out[:, cols] = (
-            mixed[:, cols].astype(F32)
-            + (dot(main_hi, body) + dot(on(here, gates_hi), last))
-            + (dot(main_lo, body) + dot(on(here, gates_lo), last))
-        ).astype(BF)
+    def take(g):
+        @pl.loop(max(1, g * peers), (g + 1) * peers)
+        def _(k):
+            at = rx.at[k]
+            remote(at, at, t_s.at[k], t_r.at[k], (dp, back(k))).wait_recv()
+
+        mine = slice(g * peers, (g + 1) * peers)
+        start = g * group
+        xr[start : start + whole] = rx[mine, :, 0:D].reshape(whole, D)
+        extra = rx[mine, :, D : D + X].reshape(whole, X)
+        for p in range(4):
+            xr[start + whole : start + group, p * X : (p + 1) * X] = dot(unpack(p), extra).astype(BF)
+
+    def hide(g, d):
+        rows = slice(g * group, (g + 1) * group)
+        v = dot(xr[rows], win_all[d])
+        hidden[d, rows] = (0.5 * v * (1.0 + jnp.tanh(0.5 * v))).astype(BF)
+
+    def answer(g, h):
+        rows = slice(g * group, (g + 1) * group)
+
+        @pl.loop(0, 2 * NY)
+        def _(d):
+            partial = dot(hidden[d, rows], wout_all[h, d])
+
+            @pl.when(d == 0)
+            def _():
+                acc[...] = partial
+
+            @pl.when(d > 0)
+            def _():
+                acc[...] += partial
+
+        mine = slice(g * peers, (g + 1) * peers)
+        ry[h, mine, :, 0:H] = acc[0:whole].astype(BF).reshape(peers, R, H)
+        packed = None
+        for p in range(4):
+            piece = lax.dot_general(
+                unpack(p),
+                acc[whole:group, p * 128 : (p + 1) * 128].astype(BF),
+                (((0,), (0,)), ((), ())),
+                preferred_element_type=F32,
+            )
+            packed = piece if packed is None else packed + piece
+        ry[h, mine, :, H : H + 128] = packed.astype(BF).reshape(peers, R, 128)
+
+        @pl.loop(max(1, g * peers), (g + 1) * peers)
+        def _(k):
+            give_back(k, h).start()
+
+        if g == 0:
+            fx[h, ex] = ry[h, 0]
+
+    chunk_out[0].relay()
+    take(0)
+    hide(0, dp)
+    chunk_in.from_sib()
+    for d in (sib, left, right, of_sib(left), of_sib(right)):
+        hide(0, d)
+    chunk_in.relay_far()
+    chunk_out[1].relay()
+    hide(0, far)
+    chunk_in.far_from_sib()
+    hide(0, of_sib(far))
+    chunk_out[0].relay_far()
+    take(1)
+    for d in (dp, sib, left, right, of_sib(left), of_sib(right), far, of_sib(far)):
+        hide(1, d)
+    chunk_out[0].from_sib()
+    chunk_out[0].far_from_sib()
+    answer(0, 0)
+    chunk_out[1].relay_far()
+    answer(1, 0)
+    chunk_out[1].from_sib()
+    chunk_out[1].far_from_sib()
+    answer(0, 1)
+    answer(1, 1)
+
+    for h in range(2):
+
+        @pl.loop(1, NE)
+        def _(k):
+            got_back(k, h).wait_recv()
+
+        body = fx[h, :, :, 0:H].reshape(rows, H)
+        last = fx[h, :, :, H : H + 128].reshape(rows, 128)
+        main = dot(weigh[0], body) + dot(weigh[1], body)
+        for p in range(4):
+            cols = slice(h * H + p * 128, h * H + (p + 1) * 128)
+            out[:, cols] = (
+                mixed[:, cols].astype(F32)
+                + main[:, p * 128 : (p + 1) * 128]
+                + (dot(weigh[2 + 2 * p], last) + dot(weigh[3 + 2 * p], last))
+            ).astype(BF)
 
     @pl.loop(1, NE)
     def _(k):
         send_out(k).wait_send()
-        give_back(k).wait_send()
-
-    for copy in weights + [swap, share, give_wo, give_ctx]:
+        give_back(k, 0).wait_send()
+        give_back(k, 1).wait_send()
+
+    for copy in sent + [swap, share, give_wo, give_ctx]:
         copy.wait_send()
 
     def finish(small, large):
@@ -551,25 +615,27 @@
             pltpu.VMEM((F, D), BF),
             pltpu.VMEM((NE, R, D + X), BF),
             pltpu.VMEM((NE, R, D + X), BF),
-            pltpu.VMEM((NE, R, D + X), BF),
-            pltpu.VMEM((NE, R, D + X), BF),
+            pltpu.VMEM((2, NE, R, H + 128), BF),
+            pltpu.VMEM((2, NE, R, H + 128), BF),
             pltpu.VMEM((NE * CAP, D), BF),
-            pltpu.VMEM((NE * CAP, D), F32),
+            pltpu.VMEM((2 * NY, NE * CAP, H), BF),
+            pltpu.VMEM((NE // 2 * CAP, H), F32),
             pltpu.VMEM((2 * NY, D, H), BF),
-            pltpu.VMEM((2 * NY, H, D), BF),
+            pltpu.VMEM((2, 2 * NY, H, H), BF),
+            pltpu.VMEM((10, F, rows), BF),
             pltpu.VMEM((rows, F), BF),
             pltpu.VMEM((rows, F), BF),
-            dma((36,)),
-            dma((36,)),
-            dma((14,)),
-            dma((14,)),
+            dma((48,)),
+            dma((48,)),
+            dma((27,)),
+            dma((27,)),
             dma((4,)),
             dma((4,)),
             dma((NE,)),
             dma((NE,)),
-            dma((NE,)),
-            dma((NE,)),
-            dma((4,)),
+            dma((2 * NE,)),
+            dma((2 * NE,)),
+            dma((5,)),
         ],
         compiler_params=pltpu.CompilerParams(
             collective_id=0, has_side_effects=True, vmem_limit_bytes=60 * 2**20

time: 156 us -> 133 us (0.85)
  Pallas kernels: 154 us -> 131 us
    pallas_call x1, Pallas kernels: 154 us -> 131 us  [body(): pl.pallas_call(kernel, out_shape=jax.ShapeDtypeStruct((F, D), BF), in_spe...]
where the time goes in v3:
time: 133 us
  Pallas kernels  131 us (98%)
  local copies, waits for them, and re-layouts  1.87 us (1%)
    pallas_call x1, Pallas kernels, body(): pl.pallas_call(kernel, out_shape=jax.ShapeDtypeStruct((F, D), BF), in_spe...  131 us

profile of v3, /device:TPU:1, one launch (start us, length us, event | category | flops | bytes accessed | tf_op | source)
XLA Modules:
  0.0 133.3 jit_solution(14553900675729889059)
XLA Ops:
  0.0 131.4 %shard_map.91 = bf16[256,1024]{1,0:T(8,128)(2,1)} custom-call(s32[2,128]{1,0:T(2,128)} %bitcast.15, s32[2,256]{1,0:T(2,128)} %bitcast.14, f32[2,1024]{1,0:T(2,128)} %gains.1, f32[32,1024]{1,0:T(8,128)} %bitcast.13, bf16[256,1024]{1,0:T(8,128)(2,1)} %bitcast.12, bf16[3,32,1024]{2,1,0:T(8,128)(2,1)} %qkv.1, bf16[32,1024]{1,0:T(8,128)(2,1)} %wo.1, ...), custom_call_target="tpu_custom_call" | custom-call | flops 14000000000 | bytes 8388608 | tf_op jit(solution)/shard_map/pallas_call | solution.py:601
  131.5 1.9 %copy.11 = bf16[1,256,1024]{2,1,0:T(8,128)(2,1)} copy(bf16[1,256,1024]{2,1,0:T(8,128)(2,1)} %bitcast.9) | data formatting | bytes 1048576

commit v4 on v3

--- a/solution.py
+++ b/solution.py
@@ -86,6 +86,7 @@
     f_s,
     f_r,
     loc,
+    line,
 ):
     dp = lax.axis_index("dp")
     ex = lax.axis_index("expert")
@@ -117,12 +118,12 @@
     def greet(to):
         pl.semaphore_signal(barrier, inc=1, device_id=to, device_id_type=MESH)
 
-    for to in (at_y(1), at_y(-1), at_y(2), sib):
+    for to in (sib, at_y(1), at_y(-1), at_y(2)):
         greet((to, ex))
-
-    @pl.loop(1, NE)
-    def _(k):
-        greet((dp, lax.rem(ex + k, NE)))
+    for step in range(1, NX):
+        greet((dp, z * NX + at_x(step)))
+    for step in range(1, NZ):
+        greet((dp, at_z(step) * NX + x))
 
     half = pl.ds(pl.multiple_of(c * H, 128), H)
     mine = [
@@ -134,7 +135,9 @@
     ]
     for copy in mine:
         copy.start()
-    pl.semaphore_wait(barrier, NE - 1 + 4)
+    pl.semaphore_wait(barrier, NX - 1 + NZ - 1 + 4)
+    for step in range(1, NX):
+        pl.semaphore_signal(line, inc=1, device_id=(dp, z * NX + at_x(step)), device_id_type=MESH)
 
     swap = remote(frames, pbuf, m_s.at[0], m_r.at[0], (at_y(2), ex))
     swap.start()
@@ -407,22 +410,24 @@
 
     def send_out(k):
         to = away(k)
-        return remote(tx.at[to], rx.at[k], t_s.at[k], t_r.at[k], (dp, to))
+        return remote(tx.at[to], rx.at[k], t_s.at[0], t_r.at[lax.div(k, NE // 2)], (dp, to))
 
     def give_back(k, h):
         to = back(k)
-        return remote(ry.at[h, k], fx.at[h, ex], f_s.at[h * NE + k], f_r.at[h * NE + k], (dp, to))
-
-    def got_back(k, h):
-        src = away(k)
-        at = fx.at[h, src]
-        return remote(at, at, f_s.at[h * NE + k], f_r.at[h * NE + k], (dp, src))
+        return remote(ry.at[h, k], fx.at[h, ex], f_s.at[h], f_r.at[h], (dp, to))
+
+    def all_of(ref, send, recv):
+        return remote(ref, ref, send, recv, (sib, ex))
+
+    pl.semaphore_wait(line, NX - 1)
 
     @pl.loop(1, NE)
     def _(k):
         send_out(k).start()
 
     rx[0] = tx[ex]
+
+    chunk_in.relay()
 
     r0 = router[...].astype(BF)
     r1 = (router[...] - r0.astype(F32)).astype(BF)
@@ -466,8 +471,6 @@
         weigh[2 + 2 * p] = on(here, gates_hi)
         weigh[3 + 2 * p] = on(here, gates_lo)
 
-    chunk_in.relay()
-    chunk_out[1].own()
 
     peers = NE // 2
     whole, more = peers * R, peers * 4
@@ -480,11 +483,8 @@
         )
 
     def take(g):
-        @pl.loop(max(1, g * peers), (g + 1) * peers)
-        def _(k):
-            at = rx.at[k]
-            remote(at, at, t_s.at[k], t_r.at[k], (dp, back(k))).wait_recv()
-
+        first = max(1, g * peers)
+        all_of(rx.at[pl.ds(first, (g + 1) * peers - first)], t_s.at[0], t_r.at[g]).wait_recv()
         mine = slice(g * peers, (g + 1) * peers)
         start = g * group
         xr[start : start + whole] = rx[mine, :, 0:D].reshape(whole, D)
@@ -495,23 +495,12 @@
     def hide(g, d):
         rows = slice(g * group, (g + 1) * group)
         v = dot(xr[rows], win_all[d])
-        hidden[d, rows] = (0.5 * v * (1.0 + jnp.tanh(0.5 * v))).astype(BF)
+        hidden[rows, pl.ds(pl.multiple_of(d * H, 128), H)] = (0.5 * v * (1.0 + jnp.tanh(0.5 * v))).astype(BF)
 
     def answer(g, h):
         rows = slice(g * group, (g + 1) * group)
 
-        @pl.loop(0, 2 * NY)
-        def _(d):
-            partial = dot(hidden[d, rows], wout_all[h, d])
-
-            @pl.when(d == 0)
-            def _():
-                acc[...] = partial
-
-            @pl.when(d > 0)
-            def _():
-                acc[...] += partial
-
+        acc[...] = dot(hidden[rows], wout_all[h].reshape(2 * NY * H, H))
         mine = slice(g * peers, (g + 1) * peers)
         ry[h, mine, :, 0:H] = acc[0:whole].astype(BF).reshape(peers, R, H)
         packed = None
@@ -532,37 +521,47 @@
         if g == 0:
             fx[h, ex] = ry[h, 0]
 
+    def sent_all():
+        for copy in sent + [swap, share, give_wo, give_ctx]:
+            copy.wait_send()
+
+        def finish(small, large):
+            for ring in small + large:
+                ring.finish()
+
+        on_both(finish)
+        all_of(tx.at[pl.ds(0, NE - 1)], t_s.at[0], t_r.at[0]).wait_send()
+
     chunk_out[0].relay()
+    chunk_out[1].own()
     take(0)
     hide(0, dp)
     chunk_in.from_sib()
     for d in (sib, left, right, of_sib(left), of_sib(right)):
         hide(0, d)
     chunk_in.relay_far()
-    chunk_out[1].relay()
     hide(0, far)
     chunk_in.far_from_sib()
     hide(0, of_sib(far))
     chunk_out[0].relay_far()
+    chunk_out[0].from_sib()
+    chunk_out[0].far_from_sib()
+    answer(0, 0)
     take(1)
     for d in (dp, sib, left, right, of_sib(left), of_sib(right), far, of_sib(far)):
         hide(1, d)
-    chunk_out[0].from_sib()
-    chunk_out[0].far_from_sib()
-    answer(0, 0)
+    chunk_out[1].relay()
+    answer(1, 0)
     chunk_out[1].relay_far()
-    answer(1, 0)
     chunk_out[1].from_sib()
     chunk_out[1].far_from_sib()
     answer(0, 1)
     answer(1, 1)
+    sent_all()
 
     for h in range(2):
 
-        @pl.loop(1, NE)
-        def _(k):
-            got_back(k, h).wait_recv()
-
+        all_of(fx.at[h, pl.ds(0, NE - 1)], f_s.at[h], f_r.at[h]).wait_recv()
         body = fx[h, :, :, 0:H].reshape(rows, H)
         last = fx[h, :, :, H : H + 128].reshape(rows, 128)
         main = dot(weigh[0], body) + dot(weigh[1], body)
@@ -574,21 +573,7 @@
                 + (dot(weigh[2 + 2 * p], last) + dot(weigh[3 + 2 * p], last))
             ).astype(BF)
 
-    @pl.loop(1, NE)
-    def _(k):
-        send_out(k).wait_send()
-        give_back(k, 0).wait_send()
-        give_back(k, 1).wait_send()
-
-    for copy in sent + [swap, share, give_wo, give_ctx]:
-        copy.wait_send()
-
-    def finish(small, large):
-        for ring in small + large:
-            ring.finish()
-
-    on_core(0, finish)
-    on_core(1, finish)
+        all_of(ry.at[h, pl.ds(0, NE - 1)], f_s.at[h], f_r.at[h]).wait_send()
 
 
 def body(
@@ -618,7 +603,7 @@
             pltpu.VMEM((2, NE, R, H + 128), BF),
             pltpu.VMEM((2, NE, R, H + 128), BF),
             pltpu.VMEM((NE * CAP, D), BF),
-            pltpu.VMEM((2 * NY, NE * CAP, H), BF),
+            pltpu.VMEM((NE * CAP, 2 * NY * H), BF),
             pltpu.VMEM((NE // 2 * CAP, H), F32),
             pltpu.VMEM((2 * NY, D, H), BF),
             pltpu.VMEM((2, 2 * NY, H, H), BF),
@@ -631,11 +616,12 @@
             dma((27,)),
             dma((4,)),
             dma((4,)),
-            dma((NE,)),
-            dma((NE,)),
-            dma((2 * NE,)),
-            dma((2 * NE,)),
+            dma((1,)),
+            dma((2,)),
+            dma((2,)),
+            dma((2,)),
             dma((5,)),
+            pltpu.SemaphoreType.REGULAR,
         ],
         compiler_params=pltpu.CompilerParams(
             collective_id=0, has_side_effects=True, vmem_limit_bytes=60 * 2**20

time: 133 us -> 121 us (0.910)
  Pallas kernels: 131 us -> 119 us
    pallas_call x1, Pallas kernels: 131 us -> 119 us  [body(): pl.pallas_call(kernel, out_shape=jax.ShapeDtypeStruct((F, D), BF), in_spe...]
where the time goes in v4:
time: 121 us
  Pallas kernels  119 us (98%)
  local copies, waits for them, and re-layouts  1.87 us (2%)
    pallas_call x1, Pallas kernels, body(): pl.pallas_call(kernel, out_shape=jax.ShapeDtypeStruct((F, D), BF), in_spe...  119 us

profile of v4, /device:TPU:1, one launch (start us, length us, event | category | flops | bytes accessed | tf_op | source)
XLA Modules:
  0.0 120.7 jit_solution(16272406299456246942)
XLA Ops:
  0.0 118.9 %shard_map.91 = bf16[256,1024]{1,0:T(8,128)(2,1)} custom-call(s32[2,128]{1,0:T(2,128)} %bitcast.15, s32[2,256]{1,0:T(2,128)} %bitcast.14, f32[2,1024]{1,0:T(2,128)} %gains.1, f32[32,1024]{1,0:T(8,128)} %bitcast.13, bf16[256,1024]{1,0:T(8,128)(2,1)} %bitcast.12, bf16[3,32,1024]{2,1,0:T(8,128)(2,1)} %qkv.1, bf16[32,1024]{1,0:T(8,128)(2,1)} %wo.1, ...), custom_call_target="tpu_custom_call" | custom-call | flops 14000000000 | bytes 8388608 | tf_op jit(solution)/shard_map/pallas_call | solution.py:586
  118.9 1.9 %copy.11 = bf16[1,256,1024]{2,1,0:T(8,128)(2,1)} copy(bf16[1,256,1024]{2,1,0:T(8,128)(2,1)} %bitcast.9) | data formatting | bytes 1048576

commit v5 on v4

--- a/solution.py
+++ b/solution.py
@@ -20,6 +20,7 @@
 R = 16
 CAP = 20
 X = 256
+Q = 256
 MEETINGS = 128
 epsilon = 1e-05
 
@@ -58,18 +59,21 @@
     strm,
     normed,
     wall,
-    wo_sib,
+    wo_all,
     proj,
     ctxh,
     ctxs,
     mixed,
     tx,
     rx,
-    ry,
-    fx,
+    ry0,
+    ry1,
+    fx0,
+    fx1,
     xr,
     hidden,
     acc,
+    tail_y,
     win_all,
     wout_all,
     weigh,
@@ -127,14 +131,21 @@
 
     half = pl.ds(pl.multiple_of(c * H, 128), H)
     mine = [
-        pltpu.make_async_copy(qkv.at[:, :, half], wall.at[pl.ds(0, 3), z, x], loc.at[0]),
-        pltpu.make_async_copy(wo.at[:, half], wall.at[3, z, x], loc.at[1]),
+        pltpu.make_async_copy(qkv.at[:, :, half], wall.at[:, z, x], loc.at[0]),
+        pltpu.make_async_copy(wo, wo_all.at[z, x], loc.at[1]),
         pltpu.make_async_copy(win, win_all.at[dp], loc.at[2]),
-        pltpu.make_async_copy(wout.at[:, pl.ds(0, H)], wout_all.at[0, dp], loc.at[3]),
-        pltpu.make_async_copy(wout.at[:, pl.ds(H, H)], wout_all.at[1, dp], loc.at[4]),
+    ] + [
+        pltpu.make_async_copy(wout.at[:, pl.ds(q * Q, Q)], wout_all.at[q, dp], loc.at[3 + q])
+        for q in range(4)
     ]
-    for copy in mine:
-        copy.start()
+    for i, copy in enumerate(mine):
+        if i != 1:
+            copy.start()
+
+    @pl.when(c == 1)
+    def _():
+        mine[1].start()
+
     pl.semaphore_wait(barrier, NX - 1 + NZ - 1 + 4)
     for step in range(1, NX):
         pl.semaphore_signal(line, inc=1, device_id=(dp, z * NX + at_x(step)), device_id_type=MESH)
@@ -143,14 +154,15 @@
     swap.start()
 
     class Ring:
-        def __init__(self, count, base, view, step_at, device):
-            self.last = count // 2
+        def __init__(self, count, base, view, step_at, device, width=H):
+            self.last, self.width = count // 2, width
             self.base, self.view, self.step_at, self.device = base, view, step_at, device
 
         def pair(self, step, hop):
             last = step == self.last
-            right = self.view(self.step_at(hop - step), pl.ds(0, H // 2 if last else H))
-            left = self.view(self.step_at(step - hop), pl.ds(H // 2 if last else 0, H // 2 if last else H))
+            part = self.width // 2 if last else self.width
+            right = self.view(self.step_at(hop - step), pl.ds(0, part))
+            left = self.view(self.step_at(step - hop), pl.ds(self.width - part, part))
             i = self.base + 2 * (step - 1)
             return (
                 remote(right, right, ring_s.at[i], ring_r.at[i], self.device(1)),
@@ -181,18 +193,23 @@
     def to_z(step):
         return (dp, at_z(step) * NX + x)
 
-    chunks = ((0, 1), (1, 1), (2, 1), (3, 1))
     small, large = {0: [], 1: []}, {0: [], 1: []}
-    for i, (m, n) in enumerate(chunks):
-        mats = pl.ds(m, n)
+    for i in range(3):
+        mats = i
         bx, bz = 12 * i, 12 * i + 4
         small[0].append(Ring(NX, bx, lambda k, w, mats=mats: wall.at[mats, z, k, :, w], at_x, to_x))
         large[0].append(Ring(NZ, bz, lambda k, w, mats=mats: wall.at[mats, k, :, :, w], at_z, to_z))
         small[1].append(Ring(NZ, bz, lambda k, w, mats=mats: wall.at[mats, k, x, :, w], at_z, to_z))
         large[1].append(Ring(NX, bx, lambda k, w, mats=mats: wall.at[mats, :, k, :, w], at_x, to_x))
+    small[1].append(Ring(NZ, 40, lambda k, w: wo_all.at[k, x, :, w], at_z, to_z, D))
+    large[1].append(Ring(NX, 36, lambda k, w: wo_all.at[:, k, :, w], at_x, to_x, D))
 
     mine[0].wait()
-    mine[1].wait()
+
+    @pl.when(c == 1)
+    def _():
+        mine[1].wait()
+
 
     def on_core(core, work):
         pl.when(c == core)(functools.partial(work, small[core], large[core]))
@@ -220,7 +237,7 @@
                 ring.relay(step)
         for near, wide in zip(small, large):
             near.wait(near.last)
-            if wide is not large[-1]:
+            if wide not in large[3:]:
                 wide.begin(1)
 
     on_core(0, small_to_large)
@@ -281,7 +298,7 @@
             self.wait(8, of_sib(far))
 
     chunk_in = Chunk(0, win_all, D)
-    chunk_out = [Chunk(9 * (1 + h), wout_all.at[h], H) for h in range(2)]
+    chunk_out = [Chunk(9 * (1 + q), wout_all.at[q], H) for q in range(4)]
     for copy in mine[2:]:
         copy.wait()
     chunk_in.own()
@@ -291,10 +308,8 @@
         for step in range(1, min(3, steps)):
             for ring in large[:3]:
                 ring.relay(step)
-            if step == 1:
+            if step == 1 and large[3:]:
                 large[3].begin(1)
-            else:
-                large[3].relay(step - 1)
 
     on_core(0, most)
     on_core(1, most)
@@ -315,14 +330,23 @@
         for step in range(3, large[0].last):
             for ring in large[:3]:
                 ring.relay(step)
-            large[3].relay(step - 1)
 
     def come(m, small, large):
         large[m].wait(large[m].last)
 
-    def output(steps, small, large):
-        step = steps[0] if large[3].last == NZ // 2 else steps[1]
-        large[3].relay(step)
+    def give_wo(step):
+        at = wo_all.at[:, at_x(step)]
+        i = 4 + (step + NX) % NX
+        return remote(at, at, m_s.at[i], m_r.at[i], (sib, ex))
+
+    def output(small, large):
+        large[3].relay(1)
+        for step in (0, 1, -1):
+            give_wo(step).start()
+
+    def output_end(small, large):
+        large[3].wait(2)
+        give_wo(2).start()
 
     def on_both(work):
         on_core(0, work)
@@ -339,8 +363,6 @@
         w = wall[m].reshape(D, H)
         for s in range(2):
             proj[m, s] = dot(normed[s], w).astype(BF)
-        if m == 1:
-            on_both(functools.partial(output, (3, 1)))
 
     lane = iota((F, 128), 1)
 
@@ -369,24 +391,23 @@
     def store_own(cols, value):
         ctxh[c, :, cols] = value
 
+    on_core(1, output)
     attend(1 - c, store_other)
-    on_both(functools.partial(output, (4, 2)))
-    give_wo = remote(wall.at[3], wo_sib, m_s.at[2], m_r.at[2], (sib, ex))
-    give_wo.start()
     give_ctx = remote(ctxs, ctxh.at[c], m_s.at[3], m_r.at[3], (sib, ex))
     give_ctx.start()
+    on_core(1, output_end)
     attend(c, store_own)
-    remote(wo_sib, wo_sib, m_s.at[2], m_r.at[2], (sib, ex)).wait_recv()
+
+    @pl.when(c == 0)
+    def _():
+        for step in range(NX):
+            give_wo(step).wait_recv()
+
     remote(
         ctxh.at[1 - c], ctxh.at[1 - c], m_s.at[3], m_r.at[3], (sib, ex)
     ).wait_recv()
-
-    def project(w):
-        return dot(ctxh[0], w[:H]) + dot(ctxh[1], w[H:])
-
-    other = pl.ds(pl.multiple_of((1 - c) * H, 128), H)
-    mixed[:, half] = (strm[:, half].astype(F32) + project(wall[3].reshape(D, H))).astype(BF)
-    mixed[:, other] = (strm[:, other].astype(F32) + project(wo_sib[...].reshape(D, H))).astype(BF)
+    w = wo_all[...].reshape(D, D)
+    mixed[...] = (strm[...].astype(F32) + (dot(ctxh[0], w[:H]) + dot(ctxh[1], w[H:]))).astype(BF)
     normed2 = layer_norm(mixed[...].astype(F32), gains[1:2, :]).astype(BF)
 
     tx[:, :, 0:D] = dot(pick[...], normed2).astype(BF).reshape(NE, R, D)
@@ -412,9 +433,13 @@
         to = away(k)
         return remote(tx.at[to], rx.at[k], t_s.at[0], t_r.at[lax.div(k, NE // 2)], (dp, to))
 
-    def give_back(k, h):
+    def quarter_of(even, odd, q):
+        return (odd if q % 2 else even).at[q // 2]
+
+    def give_back(k, q):
         to = back(k)
-        return remote(ry.at[h, k], fx.at[h, ex], f_s.at[h], f_r.at[h], (dp, to))
+        src, dst = quarter_of(ry0, ry1, q), quarter_of(fx0, fx1, q)
+        return remote(src.at[k], dst.at[ex], f_s.at[q], f_r.at[q], (dp, to))
 
     def all_of(ref, send, recv):
         return remote(ref, ref, send, recv, (sib, ex))
@@ -428,6 +453,7 @@
     rx[0] = tx[ex]
 
     chunk_in.relay()
+    chunk_out[1].own()
 
     r0 = router[...].astype(BF)
     r1 = (router[...] - r0.astype(F32)).astype(BF)
@@ -497,32 +523,39 @@
         v = dot(xr[rows], win_all[d])
         hidden[rows, pl.ds(pl.multiple_of(d * H, 128), H)] = (0.5 * v * (1.0 + jnp.tanh(0.5 * v))).astype(BF)
 
-    def answer(g, h):
+    def answer(g, q):
         rows = slice(g * group, (g + 1) * group)
-
-        acc[...] = dot(hidden[rows], wout_all[h].reshape(2 * NY * H, H))
+        acc[...] = dot(hidden[rows], wout_all[q].reshape(2 * NY * H, Q)).astype(BF)
         mine = slice(g * peers, (g + 1) * peers)
-        ry[h, mine, :, 0:H] = acc[0:whole].astype(BF).reshape(peers, R, H)
-        packed = None
-        for p in range(4):
-            piece = lax.dot_general(
-                unpack(p),
-                acc[whole:group, p * 128 : (p + 1) * 128].astype(BF),
-                (((0,), (0,)), ((), ())),
-                preferred_element_type=F32,
-            )
-            packed = piece if packed is None else packed + piece
-        ry[h, mine, :, H : H + 128] = packed.astype(BF).reshape(peers, R, 128)
+        ry, fx = quarter_of(ry0, ry1, q), quarter_of(fx0, fx1, q)
+        ry[mine, :, 0:Q] = acc[0:whole].reshape(peers, R, Q)
+        tail_y[g, :, q % 2 * Q : (q % 2 + 1) * Q] = acc[whole:group]
+        if q % 2:
+            packed = None
+            for p in range(4):
+                piece = lax.dot_general(
+                    unpack(p),
+                    tail_y[g, :, p * 128 : (p + 1) * 128],
+                    (((0,), (0,)), ((), ())),
+                    preferred_element_type=F32,
+                )
+                packed = piece if packed is None else packed + piece
+            ry[mine, :, Q : Q + 128] = packed.astype(BF).reshape(peers, R, 128)
 
         @pl.loop(max(1, g * peers), (g + 1) * peers)
         def _(k):
-            give_back(k, h).start()
+            give_back(k, q).start()
 
         if g == 0:
-            fx[h, ex] = ry[h, 0]
+            fx[ex] = ry[0]
+
+    def finish_far(chunk):
+        chunk.relay_far()
+        chunk.from_sib()
+        chunk.far_from_sib()
 
     def sent_all():
-        for copy in sent + [swap, share, give_wo, give_ctx]:
+        for copy in sent + [swap, share, give_ctx]:
             copy.wait_send()
 
         def finish(small, large):
@@ -530,10 +563,15 @@
                 ring.finish()
 
         on_both(finish)
+
+        @pl.when(c == 1)
+        def _():
+            for step in range(NX):
+                give_wo(step).wait_send()
+
         all_of(tx.at[pl.ds(0, NE - 1)], t_s.at[0], t_r.at[0]).wait_send()
 
     chunk_out[0].relay()
-    chunk_out[1].own()
     take(0)
     hide(0, dp)
     chunk_in.from_sib()
@@ -543,37 +581,50 @@
     hide(0, far)
     chunk_in.far_from_sib()
     hide(0, of_sib(far))
-    chunk_out[0].relay_far()
-    chunk_out[0].from_sib()
-    chunk_out[0].far_from_sib()
+    chunk_out[1].relay()
+    chunk_out[2].own()
+    chunk_out[3].own()
+    finish_far(chunk_out[0])
     answer(0, 0)
+    finish_far(chunk_out[1])
+    answer(0, 1)
     take(1)
     for d in (dp, sib, left, right, of_sib(left), of_sib(right), far, of_sib(far)):
         hide(1, d)
-    chunk_out[1].relay()
+    chunk_out[2].relay()
     answer(1, 0)
-    chunk_out[1].relay_far()
-    chunk_out[1].from_sib()
-    chunk_out[1].far_from_sib()
-    answer(0, 1)
     answer(1, 1)
+    chunk_out[3].relay()
+    finish_far(chunk_out[2])
+    answer(0, 2)
+    answer(1, 2)
+    finish_far(chunk_out[3])
+    answer(0, 3)
+    answer(1, 3)
     sent_all()
 
+    def wait_for(q):
+        at = quarter_of(fx0, fx1, q).at[pl.ds(0, NE - 1)]
+        all_of(at, f_s.at[q], f_r.at[q]).wait_recv()
+
     for h in range(2):
-
-        all_of(fx.at[h, pl.ds(0, NE - 1)], f_s.at[h], f_r.at[h]).wait_recv()
-        body = fx[h, :, :, 0:H].reshape(rows, H)
-        last = fx[h, :, :, H : H + 128].reshape(rows, 128)
-        main = dot(weigh[0], body) + dot(weigh[1], body)
+        main = []
+        for q in (2 * h, 2 * h + 1):
+            wait_for(q)
+            body = quarter_of(fx0, fx1, q)[:, :, 0:Q].reshape(rows, Q)
+            main.append(dot(weigh[0], body) + dot(weigh[1], body))
+        last = fx1[h, :, :, Q : Q + 128].reshape(rows, 128)
         for p in range(4):
             cols = slice(h * H + p * 128, h * H + (p + 1) * 128)
             out[:, cols] = (
                 mixed[:, cols].astype(F32)
-                + main[:, p * 128 : (p + 1) * 128]
+                + main[p // 2][:, p % 2 * 128 : (p % 2 + 1) * 128]
                 + (dot(weigh[2 + 2 * p], last) + dot(weigh[3 + 2 * p], last))
             ).astype(BF)
 
-        all_of(ry.at[h, pl.ds(0, NE - 1)], f_s.at[h], f_r.at[h]).wait_send()
+    for q in range(4):
+        at = quarter_of(ry0, ry1, q).at[pl.ds(0, NE - 1)]
+        all_of(at, f_s.at[q], f_r.at[q]).wait_send()
 
 
 def body(
@@ -592,35 +643,38 @@
             pltpu.VMEM((F, D), BF),
             pltpu.VMEM((F, D), BF),
             pltpu.VMEM((2, F, D), BF),
-            pltpu.VMEM((4, NZ, NX, D // NE, H), BF),
-            pltpu.VMEM((NZ, NX, D // NE, H), BF),
+            pltpu.VMEM((3, NZ, NX, D // NE, H), BF),
+            pltpu.VMEM((NZ, NX, D // NE, D), BF),
             pltpu.VMEM((3, 2, F, H), BF),
             pltpu.VMEM((2, F, H), BF),
             pltpu.VMEM((F, H), BF),
             pltpu.VMEM((F, D), BF),
             pltpu.VMEM((NE, R, D + X), BF),
             pltpu.VMEM((NE, R, D + X), BF),
-            pltpu.VMEM((2, NE, R, H + 128), BF),
-            pltpu.VMEM((2, NE, R, H + 128), BF),
+            pltpu.VMEM((2, NE, R, Q), BF),
+            pltpu.VMEM((2, NE, R, Q + 128), BF),
+            pltpu.VMEM((2, NE, R, Q), BF),
+            pltpu.VMEM((2, NE, R, Q + 128), BF),
             pltpu.VMEM((NE * CAP, D), BF),
             pltpu.VMEM((NE * CAP, 2 * NY * H), BF),
-            pltpu.VMEM((NE // 2 * CAP, H), F32),
+            pltpu.VMEM((NE // 2 * CAP, Q), BF),
+            pltpu.VMEM((2, NE // 2 * 4, H), BF),
             pltpu.VMEM((2 * NY, D, H), BF),
-            pltpu.VMEM((2, 2 * NY, H, H), BF),
+            pltpu.VMEM((4, 2 * NY, H, Q), BF),
             pltpu.VMEM((10, F, rows), BF),
             pltpu.VMEM((rows, F), BF),
             pltpu.VMEM((rows, F), BF),
             dma((48,)),
             dma((48,)),
-            dma((27,)),
-            dma((27,)),
+            dma((45,)),
+            dma((45,)),
+            dma((8,)),
+            dma((8,)),
+            dma((1,)),
+            dma((2,)),
             dma((4,)),
             dma((4,)),
-            dma((1,)),
-            dma((2,)),
-            dma((2,)),
-            dma((2,)),
-            dma((5,)),
+            dma((7,)),
             pltpu.SemaphoreType.REGULAR,
         ],
         compiler_params=pltpu.CompilerParams(

time: 121 us -> 126 us (1.041)
  Pallas kernels: 119 us -> 124 us
    pallas_call x1, Pallas kernels: 119 us -> 124 us  [body(): pl.pallas_call(kernel, out_shape=jax.ShapeDtypeStruct((F, D), BF), in_spe...]
where the time goes in v5:
time: 126 us; the launch traced here: 125 us
  Pallas kernels  124 us (98%)
  local copies, waits for them, and re-layouts  1.87 us (1%)
    pallas_call x1, Pallas kernels, body(): pl.pallas_call(kernel, out_shape=jax.ShapeDtypeStruct((F, D), BF), in_spe...  124 us

profile of v5, /device:TPU:1, one launch (start us, length us, event | category | flops | bytes accessed | tf_op | source)
XLA Modules:
  0.0 125.4 jit_solution(2690182744875066567)
XLA Ops:
  0.0 123.6 %shard_map.91 = bf16[256,1024]{1,0:T(8,128)(2,1)} custom-call(s32[2,128]{1,0:T(2,128)} %bitcast.15, s32[2,256]{1,0:T(2,128)} %bitcast.14, f32[2,1024]{1,0:T(2,128)} %gains.1, f32[32,1024]{1,0:T(8,128)} %bitcast.13, bf16[256,1024]{1,0:T(8,128)(2,1)} %bitcast.12, bf16[3,32,1024]{2,1,0:T(8,128)(2,1)} %qkv.1, bf16[32,1024]{1,0:T(8,128)(2,1)} %wo.1, ...), custom_call_target="tpu_custom_call" | custom-call | flops 14000000000 | bytes 8388608 | tf_op jit(solution)/shard_map/pallas_call | solution.py:637
  123.6 1.9 %copy.11 = bf16[1,256,1024]{2,1,0:T(8,128)(2,1)} copy(bf16[1,256,1024]{2,1,0:T(8,128)(2,1)} %bitcast.9) | data formatting | bytes 1048576

commit v6 on v4

--- a/solution.py
+++ b/solution.py
@@ -20,6 +20,7 @@
 R = 16
 CAP = 20
 X = 256
+Q = 256
 MEETINGS = 128
 epsilon = 1e-05
 
@@ -65,13 +66,19 @@
     mixed,
     tx,
     rx,
-    ry,
-    fx,
+    ry0,
+    ry1,
+    ry2,
+    fx0,
+    fx1,
+    fx2,
     xr,
     hidden,
     acc,
+    tail_y,
     win_all,
-    wout_all,
+    wout_a,
+    wout_b,
     weigh,
     pick,
     pick_x,
@@ -130,8 +137,9 @@
         pltpu.make_async_copy(qkv.at[:, :, half], wall.at[pl.ds(0, 3), z, x], loc.at[0]),
         pltpu.make_async_copy(wo.at[:, half], wall.at[3, z, x], loc.at[1]),
         pltpu.make_async_copy(win, win_all.at[dp], loc.at[2]),
-        pltpu.make_async_copy(wout.at[:, pl.ds(0, H)], wout_all.at[0, dp], loc.at[3]),
-        pltpu.make_async_copy(wout.at[:, pl.ds(H, H)], wout_all.at[1, dp], loc.at[4]),
+        pltpu.make_async_copy(wout.at[:, pl.ds(0, H)], wout_a.at[dp], loc.at[3]),
+        pltpu.make_async_copy(wout.at[:, pl.ds(H, Q)], wout_b.at[0, dp], loc.at[4]),
+        pltpu.make_async_copy(wout.at[:, pl.ds(H + Q, Q)], wout_b.at[1, dp], loc.at[5]),
     ]
     for copy in mine:
         copy.start()
@@ -223,8 +231,6 @@
             if wide is not large[-1]:
                 wide.begin(1)
 
-    on_core(0, small_to_large)
-    on_core(1, small_to_large)
 
     right, left, far = at_y(1), at_y(-1), at_y(2)
 
@@ -281,10 +287,12 @@
             self.wait(8, of_sib(far))
 
     chunk_in = Chunk(0, win_all, D)
-    chunk_out = [Chunk(9 * (1 + h), wout_all.at[h], H) for h in range(2)]
+    chunk_out = [Chunk(9, wout_a, H), Chunk(18, wout_b.at[0], H), Chunk(27, wout_b.at[1], H)]
     for copy in mine[2:]:
         copy.wait()
     chunk_in.own()
+    on_core(0, small_to_large)
+    on_core(1, small_to_large)
 
     def most(small, large):
         steps = large[0].last
@@ -412,9 +420,11 @@
         to = away(k)
         return remote(tx.at[to], rx.at[k], t_s.at[0], t_r.at[lax.div(k, NE // 2)], (dp, to))
 
-    def give_back(k, h):
+    ry, fx = (ry0, ry1, ry2), (fx0, fx1, fx2)
+
+    def give_back(k, q):
         to = back(k)
-        return remote(ry.at[h, k], fx.at[h, ex], f_s.at[h], f_r.at[h], (dp, to))
+        return remote(ry[q].at[k], fx[q].at[ex], f_s.at[q], f_r.at[q], (dp, to))
 
     def all_of(ref, send, recv):
         return remote(ref, ref, send, recv, (sib, ex))
@@ -497,29 +507,38 @@
         v = dot(xr[rows], win_all[d])
         hidden[rows, pl.ds(pl.multiple_of(d * H, 128), H)] = (0.5 * v * (1.0 + jnp.tanh(0.5 * v))).astype(BF)
 
-    def answer(g, h):
+    def answer(g, q):
         rows = slice(g * group, (g + 1) * group)
-
-        acc[...] = dot(hidden[rows], wout_all[h].reshape(2 * NY * H, H))
         mine = slice(g * peers, (g + 1) * peers)
-        ry[h, mine, :, 0:H] = acc[0:whole].astype(BF).reshape(peers, R, H)
-        packed = None
-        for p in range(4):
-            piece = lax.dot_general(
-                unpack(p),
-                acc[whole:group, p * 128 : (p + 1) * 128].astype(BF),
-                (((0,), (0,)), ((), ())),
-                preferred_element_type=F32,
-            )
-            packed = piece if packed is None else packed + piece
-        ry[h, mine, :, H : H + 128] = packed.astype(BF).reshape(peers, R, 128)
+        wide = H if q == 0 else Q
+        w = wout_a[...] if q == 0 else wout_b[q - 1]
+        acc[:, 0:wide] = dot(hidden[rows], w.reshape(2 * NY * H, wide)).astype(BF)
+        ry[q][mine, :, 0:wide] = acc[0:whole, 0:wide].reshape(peers, R, wide)
+        start = Q if q == 2 else 0
+        tail_y[g, :, start : start + wide] = acc[whole:group, 0:wide]
+        if q != 1:
+            packed = None
+            for p in range(4):
+                piece = lax.dot_general(
+                    unpack(p),
+                    tail_y[g, :, p * 128 : (p + 1) * 128],
+                    (((0,), (0,)), ((), ())),
+                    preferred_element_type=F32,
+                )
+                packed = piece if packed is None else packed + piece
+            ry[q][mine, :, wide : wide + 128] = packed.astype(BF).reshape(peers, R, 128)
 
         @pl.loop(max(1, g * peers), (g + 1) * peers)
         def _(k):
-            give_back(k, h).start()
+            give_back(k, q).start()
 
         if g == 0:
-            fx[h, ex] = ry[h, 0]
+            fx[q][ex] = ry[q][0]
+
+    def finish_far(chunk):
+        chunk.relay_far()
+        chunk.from_sib()
+        chunk.far_from_sib()
 
     def sent_all():
         for copy in sent + [swap, share, give_wo, give_ctx]:
@@ -534,6 +553,7 @@
 
     chunk_out[0].relay()
     chunk_out[1].own()
+    chunk_out[2].own()
     take(0)
     hide(0, dp)
     chunk_in.from_sib()
@@ -543,37 +563,45 @@
     hide(0, far)
     chunk_in.far_from_sib()
     hide(0, of_sib(far))
-    chunk_out[0].relay_far()
-    chunk_out[0].from_sib()
-    chunk_out[0].far_from_sib()
+    finish_far(chunk_out[0])
     answer(0, 0)
     take(1)
+    chunk_out[1].relay()
     for d in (dp, sib, left, right, of_sib(left), of_sib(right), far, of_sib(far)):
         hide(1, d)
-    chunk_out[1].relay()
+    chunk_out[2].relay()
     answer(1, 0)
-    chunk_out[1].relay_far()
-    chunk_out[1].from_sib()
-    chunk_out[1].far_from_sib()
+    finish_far(chunk_out[1])
     answer(0, 1)
     answer(1, 1)
+    finish_far(chunk_out[2])
+    answer(0, 2)
+    answer(1, 2)
     sent_all()
 
-    for h in range(2):
-
-        all_of(fx.at[h, pl.ds(0, NE - 1)], f_s.at[h], f_r.at[h]).wait_recv()
-        body = fx[h, :, :, 0:H].reshape(rows, H)
-        last = fx[h, :, :, H : H + 128].reshape(rows, 128)
-        main = dot(weigh[0], body) + dot(weigh[1], body)
+    def wait_for(q):
+        all_of(fx[q].at[pl.ds(0, NE - 1)], f_s.at[q], f_r.at[q]).wait_recv()
+        wide = H if q == 0 else Q
+        body = fx[q][:, :, 0:wide].reshape(rows, wide)
+        return dot(weigh[0], body) + dot(weigh[1], body)
+
+    def combine(start, main, last):
         for p in range(4):
-            cols = slice(h * H + p * 128, h * H + (p + 1) * 128)
+            cols = slice(start + p * 128, start + (p + 1) * 128)
+            i = 0 if len(main) == 1 else p // 2
+            at = (p if len(main) == 1 else p % 2) * 128
             out[:, cols] = (
                 mixed[:, cols].astype(F32)
-                + main[:, p * 128 : (p + 1) * 128]
+                + main[i][:, at : at + 128]
                 + (dot(weigh[2 + 2 * p], last) + dot(weigh[3 + 2 * p], last))
             ).astype(BF)
 
-        all_of(ry.at[h, pl.ds(0, NE - 1)], f_s.at[h], f_r.at[h]).wait_send()
+    main = [wait_for(0)]
+    combine(0, main, fx0[:, :, H : H + 128].reshape(rows, 128))
+    main = [wait_for(1), wait_for(2)]
+    combine(H, main, fx2[:, :, Q : Q + 128].reshape(rows, 128))
+    for q in range(3):
+        all_of(ry[q].at[pl.ds(0, NE - 1)], f_s.at[q], f_r.at[q]).wait_send()
 
 
 def body(
@@ -600,27 +628,33 @@
             pltpu.VMEM((F, D), BF),
             pltpu.VMEM((NE, R, D + X), BF),
             pltpu.VMEM((NE, R, D + X), BF),
-            pltpu.VMEM((2, NE, R, H + 128), BF),
-            pltpu.VMEM((2, NE, R, H + 128), BF),
+            pltpu.VMEM((NE, R, H + 128), BF),
+            pltpu.VMEM((NE, R, Q), BF),
+            pltpu.VMEM((NE, R, Q + 128), BF),
+            pltpu.VMEM((NE, R, H + 128), BF),
+            pltpu.VMEM((NE, R, Q), BF),
+            pltpu.VMEM((NE, R, Q + 128), BF),
             pltpu.VMEM((NE * CAP, D), BF),
             pltpu.VMEM((NE * CAP, 2 * NY * H), BF),
-            pltpu.VMEM((NE // 2 * CAP, H), F32),
+            pltpu.VMEM((NE // 2 * CAP, H), BF),
+            pltpu.VMEM((2, NE // 2 * 4, H), BF),
             pltpu.VMEM((2 * NY, D, H), BF),
-            pltpu.VMEM((2, 2 * NY, H, H), BF),
+            pltpu.VMEM((2 * NY, H, H), BF),
+            pltpu.VMEM((2, 2 * NY, H, Q), BF),
             pltpu.VMEM((10, F, rows), BF),
             pltpu.VMEM((rows, F), BF),
             pltpu.VMEM((rows, F), BF),
             dma((48,)),
             dma((48,)),
-            dma((27,)),
-            dma((27,)),
+            dma((36,)),
+            dma((36,)),
             dma((4,)),
             dma((4,)),
             dma((1,)),
             dma((2,)),
-            dma((2,)),
-            dma((2,)),
-            dma((5,)),
+            dma((3,)),
+            dma((3,)),
+            dma((6,)),
             pltpu.SemaphoreType.REGULAR,
         ],
         compiler_params=pltpu.CompilerParams(

time: 121 us -> 118 us (0.975)
  Pallas kernels: 119 us -> 116 us
    pallas_call x1, Pallas kernels: 119 us -> 116 us  [body(): pl.pallas_call(kernel, out_shape=jax.ShapeDtypeStruct((F, D), BF), in_spe...]
where the time goes in v6:
time: 118 us
  Pallas kernels  116 us (98%)
  local copies, waits for them, and re-layouts  1.87 us (2%)
    pallas_call x1, Pallas kernels, body(): pl.pallas_call(kernel, out_shape=jax.ShapeDtypeStruct((F, D), BF), in_spe...  116 us

profile of v6, /device:TPU:1, one launch (start us, length us, event | category | flops | bytes accessed | tf_op | source)
XLA Modules:
  0.0 117.7 jit_solution(3735649464105319558)
XLA Ops:
  0.0 115.9 %shard_map.91 = bf16[256,1024]{1,0:T(8,128)(2,1)} custom-call(s32[2,128]{1,0:T(2,128)} %bitcast.15, s32[2,256]{1,0:T(2,128)} %bitcast.14, f32[2,1024]{1,0:T(2,128)} %gains.1, f32[32,1024]{1,0:T(8,128)} %bitcast.13, bf16[256,1024]{1,0:T(8,128)(2,1)} %bitcast.12, bf16[3,32,1024]{2,1,0:T(8,128)(2,1)} %qkv.1, bf16[32,1024]{1,0:T(8,128)(2,1)} %wo.1, ...), custom_call_target="tpu_custom_call" | custom-call | flops 14000000000 | bytes 8388608 | tf_op jit(solution)/shard_map/pallas_call | solution.py:614
  115.9 1.9 %copy.11 = bf16[1,256,1024]{2,1,0:T(8,128)(2,1)} copy(bf16[1,256,1024]{2,1,0:T(8,128)(2,1)} %bitcast.9) | data formatting | bytes 1048576

commit v7 on v6

--- a/solution.py
+++ b/solution.py
@@ -220,7 +220,9 @@
     rank = dot(spread, rank)
     slot = iota((rows, F), 0)
     pick[...] = onehot(rank == lax.rem(slot, R).astype(F32))
-    pick_x[...] = onehot(rank == (lax.rem(slot, 4) + R).astype(F32))
+    in_x = rank == (lax.rem(slot, 4) + R).astype(F32)
+    for p in range(4):
+        pick_x[p] = onehot(in_x & (lax.div(lax.rem(slot, R), 4) == p))
 
     def small_to_large(small, large):
         for step in range(1, small[0].last):
@@ -395,14 +397,13 @@
     other = pl.ds(pl.multiple_of((1 - c) * H, 128), H)
     mixed[:, half] = (strm[:, half].astype(F32) + project(wall[3].reshape(D, H))).astype(BF)
     mixed[:, other] = (strm[:, other].astype(F32) + project(wo_sib[...].reshape(D, H))).astype(BF)
+    chunk_in.relay()
     normed2 = layer_norm(mixed[...].astype(F32), gains[1:2, :]).astype(BF)
 
     tx[:, :, 0:D] = dot(pick[...], normed2).astype(BF).reshape(NE, R, D)
-    tail = dot(pick_x[...], normed2)
-    part = lax.div(lax.rem(iota((rows, X), 0), R), 4)
-    packed = tail[:, 0:X]
+    packed = dot(pick_x[0], normed2[:, 0:X])
     for p in range(1, 4):
-        packed = jnp.where(part == p, tail[:, p * X : (p + 1) * X], packed)
+        packed += dot(pick_x[p], normed2[:, p * X : (p + 1) * X])
     tx[:, :, D : D + X] = packed.astype(BF).reshape(NE, R, X)
 
     def in_z(k):
@@ -436,8 +437,6 @@
         send_out(k).start()
 
     rx[0] = tx[ex]
-
-    chunk_in.relay()
 
     r0 = router[...].astype(BF)
     r1 = (router[...] - r0.astype(F32)).astype(BF)
@@ -643,7 +642,7 @@
             pltpu.VMEM((2, 2 * NY, H, Q), BF),
             pltpu.VMEM((10, F, rows), BF),
             pltpu.VMEM((rows, F), BF),
-            pltpu.VMEM((rows, F), BF),
+            pltpu.VMEM((4, rows, F), BF),
             dma((48,)),
             dma((48,)),
             dma((36,)),

time: 118 us -> 118 us (level)
  no operation moved by 1% of the time
where the time goes in v7:
time: 118 us
  Pallas kernels  116 us (98%)
  local copies, waits for them, and re-layouts  1.87 us (2%)
    pallas_call x1, Pallas kernels, body(): pl.pallas_call(kernel, out_shape=jax.ShapeDtypeStruct((F, D), BF), in_spe...  116 us

profile of v7, /device:TPU:1, one launch (start us, length us, event | category | flops | bytes accessed | tf_op | source)
XLA Modules:
  0.0 117.7 jit_solution(16013643360352978537)
XLA Ops:
  0.0 115.8 %shard_map.91 = bf16[256,1024]{1,0:T(8,128)(2,1)} custom-call(s32[2,128]{1,0:T(2,128)} %bitcast.15, s32[2,256]{1,0:T(2,128)} %bitcast.14, f32[2,1024]{1,0:T(2,128)} %gains.1, f32[32,1024]{1,0:T(8,128)} %bitcast.13, bf16[256,1024]{1,0:T(8,128)(2,1)} %bitcast.12, bf16[3,32,1024]{2,1,0:T(8,128)(2,1)} %qkv.1, bf16[32,1024]{1,0:T(8,128)(2,1)} %wo.1, ...), custom_call_target="tpu_custom_call" | custom-call | flops 14000000000 | bytes 8388608 | tf_op jit(solution)/shard_map/pallas_call | solution.py:613
  115.8 1.9 %copy.11 = bf16[1,256,1024]{2,1,0:T(8,128)(2,1)} copy(bf16[1,256,1024]{2,1,0:T(8,128)(2,1)} %bitcast.9) | data formatting | bytes 1048576
